TPU v7x, 1024 devices: a whole 8x8x8 slice. The times are simulated.
1024 devices in a mesh: blk: 256 (over z_lo, y, x, core), rep: 4 (over z_hi).
Axes of the slice: x: 8, y: 8, z: 8 (z_hi: 4, z_lo: 2; z = z_hi * 2 + z_lo), core: 2. Of those that a mesh axis runs over, the one named last changes fastest.
Arguments:
- features: bfloat16 [65536, 768], P('blk', 'rep'), may hold values from -6 to 6
- weight: bfloat16 [768, 1024], replicated, may hold values from -0.21875 to 0.21875
- cotangent: bfloat16 [65536, 1024], P('blk', 'rep'), may hold values from -6 to 6
- tile_val: bfloat16 [256, 20, 128, 128], P('blk'), may hold values from -40 to 40
- tile_row: int32 [256, 20], P('blk'), may hold values from 0 to 1
- tile_col: int32 [256, 20], P('blk'), may hold values from 0 to 17
- tile_count: int32 [256], P('blk'), may hold values from 2 to 20, as said below
Outputs:
- hidden: bfloat16 [65536, 1024], P('blk', 'rep')
- weight_grad: float32 [768, 1024], P('rep')
- feature_grad: bfloat16 [65536, 768], P('blk', 'rep')
Inputs may be any that keep to these rules, and one draw needn't show every extreme that they name: Slots from tile_count[b] on are ignored; some block fills all 20 slots.
All inputs are finite; a program needn't handle non-finite values.
Results may differ from a plain program's by a relative error of at most 0.015.
Values may be sent and summed in bfloat16 or wider, within the bound.
A program may use at most 32 MiB of HBM per device.

v0:
```python
import jax
import jax.numpy as jnp
from jax import lax
from jax.sharding import PartitionSpec as P

TILE = 128
ROWT = 2
REACH = 4


def passed_along(value, axis, steps):
    count = lax.axis_size(axis)
    pairs = [(source, (source + steps) % count) for source in range(count)]
    return lax.ppermute(value, axis, pairs)


def dsilu(value):
    sig = jax.nn.sigmoid(value)
    return sig * (1.0 + value * (1.0 - sig))


def body(features, weight, cotangent, tile_val, tile_row, tile_col, tile_count):
    highest = lax.Precision.HIGHEST
    rows_dev, panel = features.shape
    slots = tile_val.shape[1]
    wide = (2 * REACH + 1) * ROWT
    vals = tile_val[0]
    live = (lax.iota(jnp.int32, slots) < tile_count[0]).astype(jnp.float32)
    place = (tile_row[0][None, :] == lax.iota(jnp.int32, ROWT)[:, None]).astype(jnp.float32) * live[
        None, :
    ]
    spot = (tile_col[0][None, :] == lax.iota(jnp.int32, wide)[:, None]).astype(jnp.float32) * live[
        None, :
    ]
    tile_sq = jnp.sum(jnp.square(vals.astype(jnp.float32)), axis=2)
    row_sq = jnp.dot(place, tile_sq, precision=highest)
    scale = lax.rsqrt(1.0 + row_sq.reshape(rows_dev, 1))
    pieces = []
    for offset in range(2 * REACH + 1):
        if offset == REACH:
            pieces.append(features)
        else:
            pieces.append(passed_along(features, "blk", REACH - offset))
    window = jnp.concatenate(pieces, axis=0).reshape(wide, TILE, panel)
    taken = window[tile_col[0]]
    prod = jnp.einsum("sab,sbf->saf", vals, taken, preferred_element_type=jnp.float32)
    summed = jnp.einsum("rs,saf->raf", place, prod, precision=highest)
    agg = (features.astype(jnp.float32) + scale * summed.reshape(rows_dev, panel)).astype(
        jnp.bfloat16
    )
    replica = lax.axis_index("rep")
    own_weight = lax.dynamic_slice_in_dim(weight, replica * panel, panel, 0)
    hid_part = cotangent.shape[1]
    agg_full, cot_full = (
        lax.all_gather(agg, "rep", axis=1, tiled=True),
        lax.all_gather(cotangent, "rep", axis=1, tiled=True),
    )
    pre = jnp.dot(agg_full, weight, preferred_element_type=jnp.float32)
    own_pre = lax.dynamic_slice_in_dim(pre, replica * hid_part, hid_part, 1)
    hidden = jax.nn.silu(own_pre).astype(jnp.bfloat16)
    grad_pre = (cot_full.astype(jnp.float32) * dsilu(pre)).astype(jnp.bfloat16)
    partial_grad = lax.dot_general(
        agg, grad_pre, (((0,), (0,)), ((), ())), preferred_element_type=jnp.float32
    )
    back = lax.dot_general(
        grad_pre, own_weight, (((1,), (1,)), ((), ())), preferred_element_type=jnp.float32
    )
    nodes = rows_dev * lax.axis_size("blk")
    weight_grad = lax.psum(partial_grad, "blk") / jnp.sqrt(jnp.float32(nodes))
    scaled = (scale * back).astype(jnp.bfloat16).reshape(ROWT, TILE, panel)
    rows_in = scaled[tile_row[0]]
    contrib = jnp.einsum("sab,saf->sbf", vals, rows_in, preferred_element_type=jnp.float32)
    parts = jnp.einsum("ws,sbf->wbf", spot, contrib, precision=highest).reshape(
        2 * REACH + 1, rows_dev, panel
    )
    total = parts[REACH]
    for offset in range(2 * REACH + 1):
        if offset != REACH:
            total = total + passed_along(
                parts[offset].astype(jnp.bfloat16), "blk", offset - REACH
            ).astype(jnp.float32)
    feature_grad = (back + total).astype(jnp.bfloat16)
    return (hidden, weight_grad, feature_grad)


def solution(mesh):
    placed = (
        P("blk", "rep"),
        P(),
        P("blk", "rep"),
        P("blk", None, None, None),
        P("blk", None),
        P("blk", None),
        P("blk"),
    )
    return jax.shard_map(
        body,
        mesh=mesh,
        in_specs=placed,
        out_specs=(P("blk", "rep"), P("rep", None), P("blk", "rep")),
        check_vma=False,
    )
```

profile of v0, /device:TPU:1, one launch (start us, length us, event | category | flops | bytes accessed | tf_op | source)
XLA Modules:
  0.0 2071.4 jit_solution(1057117148479636792)
XLA Ops:
  7.2 0.0 copy-start
  7.2 0.0 copy-start.3
  7.2 0.0 all-reduce.2.cloned.1.call-start
  7.2 12.4 collective-permute-start.6
  19.7 3.1 collective-permute-start.5
  22.8 4.5 collective-permute-start.4
  27.3 3.5 collective-permute-start.3
  30.9 4.5 collective-permute-start
  36.1 0.7 fusion.33
  36.7 0.7 fusion.32
  37.4 1.5 multiply_reduce_fusion
  38.9 24.6 %all_gather.7 = bf16[256,1024]{1,0:T(8,128)(2,1)} all-gather(bf16[256,256]{1,0:T(8,128)(2,1)} %param.9), channel_id=1, replica_groups=mesh['blk'=256,'rep'=4] {'rep'}, dimensions={1}, use_global_device_ids=true | all-gather | bytes 655360 | tf_op jit(solution)/shard_map/all_gather | solution.py:56
  63.5 0.8 fusion.7
  64.3 0.0 collective-permute-done
  64.3 1.9 collective-permute-start.1
  66.3 8.8 collective-permute-done.1
  75.1 1.9 collective-permute-start.2
  77.0 7.8 collective-permute-done.2
  84.9 0.0 copy-done.3
  84.9 1.9 collective-permute-start.7
  86.8 0.0 collective-permute-done.3
  86.9 0.0 collective-permute-done.4
  86.9 0.0 collective-permute-done.5
  86.9 0.0 collective-permute-done.6
  86.9 5.0 collective-permute-done.7
  91.9 0.2 copy_bitcast_fusion
  92.1 0.0 copy-start.1
  92.2 1.7 gather_fusion
  93.9 1.8 fusion.10
  95.6 0.0 copy-start.2
  95.6 2.4 fusion.2
  98.1 13.1 all_gather.6
  111.2 0.0 copy-done
  111.2 1.8 multiply_convert_fusion
  113.0 1.1 fusion.46
  114.1 0.3 fusion.12
  114.5 0.0 all-reduce.2.cloned.1.call-update
  114.5 0.7 gather_fusion.1
  115.3 0.0 copy-start.5
  115.3 0.4 fusion.8
  115.7 0.2 copy-done.5
  115.9 4.4 fusion.45
  120.4 0.6 fusion.44
  121.0 10.5 collective-permute-start.9
  131.5 3.4 collective-permute-start.10
  135.0 1.9 collective-permute-start.11
  137.0 3.6 collective-permute-start.12
  140.7 1.9 collective-permute-start.13
  142.6 1.2 slice.57
  143.8 0.0 collective-permute-done.9
  143.8 1.9 collective-permute-start.14
  145.7 0.0 collective-permute-done.10
  145.7 1.9 collective-permute-start.15
  147.6 0.0 collective-permute-done.11
  147.7 8.8 collective-permute-start.8
  156.4 1.7 multiply_convert_fusion.1
  158.1 0.0 collective-permute-done.12
  158.1 0.0 collective-permute-done.13
  158.1 0.0 collective-permute-done.14
  158.1 2.8 collective-permute-done.15
  160.9 0.0 collective-permute-done.8
  160.9 0.8 fusion.22
  161.7 1900.8 %all-reduce.2.cloned.1.call-done = f32[192,1024]{1,0:T(8,128)} async-done(((f32[192,1024]{1,0:T(8,128)}), f32[192,1024]{1,0:T(8,128)}) %all-reduce.2.cloned.1.call-update) | async-done | bytes 786448 | tf_op jit(solution)/shard_map/psum | solution.py:69
  2062.5 2.1 broadcast_multiply_fusion
  (26 shorter events, 0.3 us)
Async XLA Ops:
  7.2 104.1 %copy-start = (bf16[768,1024]{1,0:T(8,128)(2,1)S(1)}, bf16[768,1024]{1,0:T(8,128)(2,1)}, u32[]{:S(2)}) copy-start(bf16[768,1024]{1,0:T(8,128)(2,1)} %param.8) | copy-start | bytes 4718596
  7.2 77.7 %copy-start.3 = (bf16[256,192]{0,1:T(8,128)(2,1)S(1)}, bf16[256,192]{0,1:T(8,128)(2,1)}, u32[]{:S(2)}) copy-start(bf16[256,192]{0,1:T(8,128)(2,1)} %param.7) | copy-start | bytes 294916
  7.2 2055.3 %all-reduce.2.cloned.1.call-start = ((), (), s32[]{:S(2)}) async-start(), calls=%async_computation | async-start | bytes 1572864 | tf_op jit(solution)/shard_map/psum | solution.py:69
  7.2 79.7 %collective-permute-start.6 = (bf16[256,192]{0,1:T(8,128)(2,1)}, bf16[256,192]{0,1:T(8,128)(2,1)S(1)}, u32[]{:S(2)}, u32[]{:S(2)}) collective-permute-start(bf16[256,192]{0,1:T(8,128)(2,1)} %param.7), channel_id=1, source_target_pairs={{0,1012},{4,1016},{8,1020},{12,0},{16,4},{20,8},{24,12},{28,16},{3... | collective-permute-start | bytes 294920 | tf_op jit(solution)/shard_map/ppermute | solution.py:14
  19.7 67.2 %collective-permute-start.5 = (bf16[256,192]{0,1:T(8,128)(2,1)}, bf16[256,192]{0,1:T(8,128)(2,1)S(1)}, u32[]{:S(2)}, u32[]{:S(2)}) collective-permute-start(bf16[256,192]{0,1:T(8,128)(2,1)} %param.7), channel_id=1, source_target_pairs={{0,1016},{4,1020},{8,0},{12,4},{16,8},{20,12},{24,16},{28,20},{32,... | collective-permute-start | bytes 294920 | tf_op jit(solution)/shard_map/ppermute | solution.py:14
  22.8 64.1 %collective-permute-start.4 = (bf16[256,192]{0,1:T(8,128)(2,1)}, bf16[256,192]{0,1:T(8,128)(2,1)S(1)}, u32[]{:S(2)}, u32[]{:S(2)}) collective-permute-start(bf16[256,192]{0,1:T(8,128)(2,1)} %param.7), channel_id=1, source_target_pairs={{0,1020},{4,0},{8,4},{12,8},{16,12},{20,16},{24,20},{28,24},{32,28... | collective-permute-start | bytes 294920 | tf_op jit(solution)/shard_map/ppermute | solution.py:14
  27.3 59.5 %collective-permute-start.3 = (bf16[256,192]{0,1:T(8,128)(2,1)}, bf16[256,192]{0,1:T(8,128)(2,1)S(1)}, u32[]{:S(2)}, u32[]{:S(2)}) collective-permute-start(bf16[256,192]{0,1:T(8,128)(2,1)} %param.7), channel_id=1, source_target_pairs={{0,4},{4,8},{8,12},{12,16},{16,20},{20,24},{24,28},{28,32},{32,36}... | collective-permute-start | bytes 294920 | tf_op jit(solution)/shard_map/ppermute | solution.py:14
  30.9 33.5 %collective-permute-start = (bf16[256,192]{0,1:T(8,128)(2,1)}, bf16[256,192]{0,1:T(8,128)(2,1)S(1)}, u32[]{:S(2)}, u32[]{:S(2)}) collective-permute-start(bf16[256,192]{0,1:T(8,128)(2,1)} %param.7), channel_id=1, source_target_pairs={{0,16},{4,20},{8,24},{12,28},{16,32},{20,36},{24,40},{28,44},{32,4... | collective-permute-start | bytes 294920 | tf_op jit(solution)/shard_map/ppermute | solution.py:14
  64.3 10.8 collective-permute-start.1
  75.1 9.8 collective-permute-start.2
  84.9 7.0 collective-permute-start.7
  92.1 1.7 copy-start.1
  93.8 1.8 copy-start.4
  95.6 15.6 copy-start.2
  115.3 0.7 copy-start.5
  121.0 22.7 %collective-permute-start.9 = (bf16[256,192]{0,1:T(8,128)(2,1)S(1)}, bf16[256,192]{0,1:T(8,128)(2,1)S(1)}, u32[]{:S(2)}, u32[]{:S(2)}) collective-permute-start(bf16[256,192]{0,1:T(8,128)(2,1)S(1)} %bitcast.149), channel_id=1, source_target_pairs={{0,1012},{4,1016},{8,1020},{12,0},{16,4},{20,8},{24,12},{28,16},{3... | collective-permute-start | bytes 294920 | tf_op jit(solution)/shard_map/ppermute | solution.py:14
  131.5 14.2 collective-permute-start.10
  135.0 12.7 collective-permute-start.11
  137.0 21.1 %collective-permute-start.12 = (bf16[256,192]{0,1:T(8,128)(2,1)S(1)}, bf16[256,192]{0,1:T(8,128)(2,1)S(1)}, u32[]{:S(2)}, u32[]{:S(2)}) collective-permute-start(bf16[256,192]{0,1:T(8,128)(2,1)S(1)} %bitcast.151), channel_id=1, source_target_pairs={{0,4},{4,8},{8,12},{12,16},{16,20},{20,24},{24,28},{28,32},{32,36}... | collective-permute-start | bytes 294920 | tf_op jit(solution)/shard_map/ppermute | solution.py:14
  140.7 17.5 collective-permute-start.13
  143.8 14.3 collective-permute-start.14
  145.7 15.2 collective-permute-start.15
  147.7 13.2 collective-permute-start.8
Sparse Core Ops, SparseCore 0:
  114.6 1947.8 all-reduce.1
where the time goes:
time: 2070 us
  waiting for transfers between devices  1930 us (93%)
  starting transfers between devices  67.9 us (3%)
  blocking collectives  37.8 us (2%)
    psum x1, waiting for transfers between devices, body(): weight_grad = lax.psum(partial_grad, 'blk') / jnp.sqrt(jnp.float32(nodes))  1900 us
    ppermute x16, starting transfers between devices, passed_along(): return lax.ppermute(value, axis, pairs)  67.8 us
  transfers between devices with their start and end apart: 17, of which 5 were waited for; matrix products, arithmetic and copies ran while one was open for 1% of the time, Pallas kernels for 0%

commit v1 on v0

v1 whole, which is shorter than its diff:
```python
import functools

import jax
import jax.numpy as jnp
from jax import lax
from jax.experimental import pallas as pl
from jax.experimental.pallas import tpu as pltpu
from jax.sharding import PartitionSpec as P

TILE = 128
ROWT = 2
REACH = 4
WIDE = 2 * REACH + 1
ZL, NY, NX, NC = 2, 8, 8, 2
SUB = 16
F32 = jnp.float32
BF16 = jnp.bfloat16


def mm(a, b):
    return jnp.dot(a, b, preferred_element_type=F32)


def mm_nt(a, b):
    return lax.dot_general(a, b, (((1,), (1,)), ((), ())), preferred_element_type=F32)


def remote(src, dst, send, recv, where):
    return pltpu.make_async_remote_copy(
        src_ref=src, dst_ref=dst, send_sem=send, recv_sem=recv,
        device_id=where, device_id_type=pl.DeviceIdType.MESH,
    )


def kernel(
    nodes, slots, reps,
    feat_hbm, weight_hbm, cot_hbm, val_hbm, row_ref, col_ref, count_ref,
    hidden_out, wgrad_out, fgrad_out,
    feat, wx, vals, win, adj, adj_t, scale, acc_lo, acc_e, acc_o,
    aggbuf, agg_t, pre, cotbuf, grad, hidden, back, sl, sh, own_part, parts, backbuf, fgrad,
    core_out, core_in, core_own, y_out, y_in, x_out, x_in, xg, yg,
    local_sem, wx_sem, halo_s, halo_r, cot_s, cot_r, agg_s, agg_r, core_s, core_r,
    y_s, y_r, x_s, x_r, xg_s, xg_r, yg_s, yg_r, cg_s, cg_r, hb_s, hb_r, out_sem,
):
    blk = lax.axis_index("blk")
    rep = lax.axis_index("rep")
    blocks = ZL * NY * NX * NC
    core = blk % NC
    x = (blk // NC) % NX
    y = (blk // (NC * NX)) % NY
    zl = blk // (NC * NX * NY)
    xz = zl * NX + x
    panel = feat.shape[1]
    low = TILE
    pieces, piece_rows, _ = core_out.shape
    x_rows = x_out.shape[1]

    def blk_at(offset):
        return {"blk": (blk + offset + blocks) % blocks}

    def y_at(step):
        return {"blk": ((zl * NY + (y + step) % NY) * NX + x) * NC + core}

    def x_at(step):
        return {"blk": ((zl * NY + y) * NX + (x + step) % NX) * NC + core}

    def xz_at(step):
        g = (xz + step) % (ZL * NX)
        return {"blk": (((g // NX) * NY + y) * NX + g % NX) * NC + core}

    def rep_at(step):
        return {"rep": (rep + step) % reps}

    sibling = {"blk": blk + 1 - 2 * core}
    offsets = [d for d in range(-REACH, REACH + 1) if d != 0]

    barrier = pltpu.get_barrier_semaphore()

    def greet(where):
        pl.semaphore_signal(barrier, inc=1, device_id=where, device_id_type=pl.DeviceIdType.MESH)

    for d in offsets:
        greet(blk_at(d))
    for step in range(1, reps):
        greet(rep_at(step))
    for step in range(1, NY):
        greet(y_at(step))
    for step in range(1, ZL * NX):
        greet(xz_at(step))
    greeted = len(offsets) + reps - 1 + NY - 1 + ZL * NX - 1

    get_feat = pltpu.make_async_copy(feat_hbm, feat, local_sem.at[0])
    get_feat.start()
    get_cot = pltpu.make_async_copy(cot_hbm, cotbuf.at[rep], local_sem.at[1])
    get_cot.start()
    get_vals = pltpu.make_async_copy(val_hbm.at[0], vals, local_sem.at[2])
    get_vals.start()
    get_wx = []
    high = panel - low
    for q in range(reps):
        get_wx.append(
            pltpu.make_async_copy(
                weight_hbm.at[pl.ds(q * panel, panel)], wx.at[q, pl.ds(0, panel)], wx_sem.at[2 * q]
            )
        )
        get_wx.append(
            pltpu.make_async_copy(
                weight_hbm.at[pl.ds(q * panel + low, high)],
                wx.at[q, pl.ds(panel, high)],
                wx_sem.at[2 * q + 1],
            )
        )
    for copy in get_wx:
        copy.start()

    get_feat.wait()
    win[REACH, 0:256, :] = feat[:, 0:low]
    win[REACH, 256:384, 0:high] = feat[0:TILE, low:panel]
    win[REACH, 256:384, high:low] = feat[TILE : 2 * TILE, low:panel]
    get_cot.wait()

    pl.semaphore_wait(barrier, greeted)

    halo = {}
    for d in (4, -4, 3, -3, 2, -2, 1, -1):
        halo[d] = remote(win.at[REACH], win.at[REACH - d], halo_s.at[d + REACH], halo_r.at[REACH - d], blk_at(d))
        halo[d].start()
    rep_steps = [2, 1, 3] if reps == 4 else list(range(1, reps))
    cots = {}
    for step in rep_steps:
        cots[step] = remote(cotbuf.at[rep], cotbuf.at[rep], cot_s.at[step], cot_r.at[step], rep_at(step))
        cots[step].start()

    get_vals.wait()
    count = count_ref[0]
    keys = []
    rows = []
    for s in range(slots):
        alive = s < count
        rows.append(jnp.where(alive, row_ref[0, s], -1))
        keys.append(jnp.where(alive, row_ref[0, s] * (WIDE * ROWT) + col_ref[0, s], -1))

    def one_where(cond):
        return jnp.where(cond, 1.0, 0.0).astype(F32)

    chunk = 32

    @pl.loop(0, TILE // chunk)
    def _(c):
        at = pl.ds(pl.multiple_of(c * chunk, chunk), chunk)
        sums = [jnp.zeros((chunk, TILE), F32) for _ in range(ROWT)]
        for s in range(slots):
            v = vals[s, at, :].astype(F32)
            sq = v * v
            for r in range(ROWT):
                sums[r] = sums[r] + sq * one_where(rows[s] == r)
        for r in range(ROWT):
            row_sq = jnp.sum(sums[r], axis=1, keepdims=True)
            to = pl.ds(pl.multiple_of(r * TILE + c * chunk, chunk), chunk)
            scale[to, :] = jnp.broadcast_to(lax.rsqrt(1.0 + row_sq), (chunk, TILE))

    @pl.loop(0, WIDE)
    def _(j):
        masks = [
            [[one_where(keys[s] == r * (WIDE * ROWT) + j * ROWT + t) for s in range(slots)] for t in range(ROWT)]
            for r in range(ROWT)
        ]

        @pl.loop(0, TILE // chunk)
        def _(c):
            at = pl.ds(pl.multiple_of(c * chunk, chunk), chunk)
            sums = [[jnp.zeros((chunk, TILE), F32) for _ in range(ROWT)] for _ in range(ROWT)]
            for s in range(slots):
                v = vals[s, at, :].astype(F32)
                for r in range(ROWT):
                    for t in range(ROWT):
                        sums[r][t] = sums[r][t] + v * masks[r][t][s]
            for r in range(ROWT):
                to = pl.ds(pl.multiple_of(r * TILE + c * chunk, chunk), chunk)
                for t in range(ROWT):
                    adj[j, to, t * TILE : (t + 1) * TILE] = sums[r][t].astype(BF16)

    for d in (0, 1, -1, 2, -2, 3, -3, 4, -4):
        j = REACH - d
        if d != 0:
            halo[d].wait_recv()
        lo = mm(adj[j], win[j, 0:256, :])
        packed = win[j, 256:384, :]
        even = mm(adj[j, :, 0:TILE], packed)
        odd = mm(adj[j, :, TILE : 2 * TILE], packed)
        if d == 0:
            acc_lo[...] = lo
            acc_e[...] = even
            acc_o[...] = odd
        else:
            acc_lo[...] += lo
            acc_e[...] += even
            acc_o[...] += odd

    left = lax.broadcasted_iota(jnp.int32, (TILE, TILE), 1) < high
    summed_lo = win[REACH, 0:256, :].astype(F32) + scale[...] * acc_lo[...]
    both = scale[...] * (acc_e[...] + pltpu.roll(acc_o[...], high, 1))
    both = jnp.where(left, both[0:TILE], pltpu.roll(both[TILE : 2 * TILE], high, 1))
    summed_hi = win[REACH, 256:384, :].astype(F32) + both
    aggbuf[rep, 0:256, :] = summed_lo.astype(BF16)
    aggbuf[rep, 256:384, :] = summed_hi.astype(BF16)
    aggs = {}
    for step in rep_steps:
        aggs[step] = remote(aggbuf.at[rep], aggbuf.at[rep], agg_s.at[step], agg_r.at[step], rep_at(step))
        aggs[step].start()

    agg_t[0:TILE, :] = summed_lo.T.astype(BF16)
    hi_t = summed_hi.T.astype(BF16)
    agg_t[TILE:panel, 0:TILE] = hi_t[0:high]
    agg_t[TILE:panel, TILE : 2 * TILE] = hi_t[high:low]

    def unpacked(q):
        p = aggbuf[q, 256:384, :].astype(F32)
        hi = jnp.concatenate([jnp.where(left, p, 0.0), jnp.where(left, 0.0, p)], axis=0).astype(BF16)
        return aggbuf[q, 0:256, :], hi

    for copy in get_wx:
        copy.wait()
    groups = pre.shape[0]
    wide = pre.shape[2]

    def add_pre(q, first):
        lo, hi = unpacked(q)
        lhs = jnp.concatenate([lo, hi], axis=1)
        for n in range(groups):
            part = mm(lhs, wx[q, :, n * wide : (n + 1) * wide])
            if first:
                pre[n] = part
            else:
                pre[n] += part

    add_pre(rep, True)

    @pl.loop(0, WIDE)
    def _(j):
        for t in range(ROWT):
            adj_t[j, :, t * 256 : (t + 1) * 256] = adj[j, :, t * TILE : (t + 1) * TILE].astype(F32).T.astype(BF16)

    for step in rep_steps[1:] + rep_steps[:1]:
        aggs[step].wait_recv()
        add_pre((rep + reps - step) % reps, False)
    for step in rep_steps:
        cots[step].wait_recv()

    def grad_at(n):
        v = pre[n]
        sig = jax.nn.sigmoid(v)
        slope = sig * (1.0 + v * (1.0 - sig))
        grad[n] = (cotbuf[n].astype(F32) * slope).astype(BF16)

    def weight_part(n, u, out):
        part = mm(agg_t[...], grad[n]).astype(out.dtype)
        for t in range(wide // TILE):
            for h in range(2):
                out[(u * (wide // TILE) + t) * 2 + h] = part[
                    h * piece_rows : (h + 1) * piece_rows, t * TILE : (t + 1) * TILE
                ]

    half = groups // 2
    for u in range(half):
        n = (1 - core) * half + u
        grad_at(n)
        weight_part(n, u, core_out)
    core_copy = remote(core_out, core_in, core_s.at[0], core_r.at[0], sibling)
    core_copy.start()
    for u in range(half):
        n = core * half + u
        grad_at(n)
        weight_part(n, u, core_own)

    back_sum = mm_nt(grad[0], wx[rep, :, 0:wide])
    for n in range(1, groups):
        back_sum = back_sum + mm_nt(grad[n], wx[rep, :, n * wide : (n + 1) * wide])
    back[...] = back_sum

    core_copy.wait_recv()
    for i in range(pieces):
        total = core_own[i] + core_in[i].astype(F32)
        core_own[i] = total
        y_out[i] = total.astype(BF16)
    ys = []
    for step in (4, 3, 5, 2, 6, 1, 7) if NY == 8 else range(1, NY):
        copy = remote(y_out.at[(y + step) % NY], y_in.at[y], y_s.at[step], y_r.at[step], y_at(step))
        copy.start()
        ys.append(copy)

    back_lo = back[:, 0:TILE]
    back_hi = back[:, TILE : 2 * TILE]
    left2 = lax.broadcasted_iota(jnp.int32, (2 * TILE, TILE), 1) < high
    scaled_hi = scale[...] * back_hi
    sl[...] = (scale[...] * back_lo).astype(BF16)
    sh[0:256, :] = jnp.where(left2, scaled_hi, 0.0).astype(BF16)
    sh[256:512, :] = jnp.where(left2, 0.0, scaled_hi).astype(BF16)

    def parts_of(j):
        at = adj_t[j]
        return mm(at[:, 0:256], sl[...]), mm(at[:, 256:512], sl[...]), mm(at, sh[...])

    hbs = []
    for d in (4, -4, 3, -3, 2, -2, 1, -1):
        j = REACH + d
        for i, part in enumerate(parts_of(j)):
            parts[j, i * TILE : (i + 1) * TILE, :] = part.astype(BF16)
        copy = remote(parts.at[j], backbuf.at[REACH - d], hb_s.at[d + REACH], hb_r.at[REACH - d], blk_at(d))
        copy.start()
        hbs.append(copy)
    a, b, c = parts_of(REACH)
    own_part[0:TILE, :] = a + back_lo[0:TILE]
    own_part[TILE : 2 * TILE, :] = b + back_lo[TILE : 2 * TILE]
    own_part[2 * TILE : 3 * TILE, :] = c + jnp.where(left, back_hi[0:TILE], back_hi[TILE : 2 * TILE])

    v = pre[rep]
    hidden[...] = (v * jax.nn.sigmoid(v)).astype(BF16)
    put_hidden = pltpu.make_async_copy(hidden, hidden_out, out_sem.at[0])
    put_hidden.start()

    for copy in ys:
        copy.wait_recv()
    total = core_own[y]
    for step in range(1, NY):
        total = total + y_in[(y + step) % NY].astype(F32)
    filled = piece_rows // x_rows
    x_out[0:filled] = total.astype(BF16).reshape(filled, x_rows, TILE)
    if filled < NX:
        x_out[filled:NX] = jnp.zeros((NX - filled, x_rows, TILE), BF16)
    xs = []
    for step in range(1, ZL * NX):
        to = ((xz + step) % (ZL * NX)) % NX
        copy = remote(x_out.at[to], x_in.at[xz], x_s.at[step], x_r.at[step], xz_at(step))
        copy.start()
        xs.append(copy)
    x_in[xz] = x_out[x]
    for copy in xs:
        copy.wait_recv()
    total = x_in[0].astype(F32)
    for g in range(1, ZL * NX):
        total = total + x_in[g].astype(F32)
    xg[x] = (total * nodes ** -0.5).astype(BF16)
    xgs = []
    for step in range(1, NX):
        copy = remote(xg.at[x], xg.at[x], xg_s.at[step], xg_r.at[step], x_at(step))
        copy.start()
        xgs.append(copy)
    for copy in xgs:
        copy.wait_recv()
    yg[y] = xg[0:filled].reshape(piece_rows, TILE)
    ygs = []
    for step in (4, 3, 5, 2, 6, 1, 7) if NY == 8 else range(1, NY):
        copy = remote(yg.at[y], yg.at[y], yg_s.at[step], yg_r.at[step], y_at(step))
        copy.start()
        ygs.append((step, copy))
    cgs = []

    def pass_on(at, step):
        copy = remote(yg.at[at], wgrad_out.at[core, at], cg_s.at[step], cg_r.at[step], sibling)
        copy.start()
        cgs.append(copy)

    pass_on(y, 0)

    for copy in hbs:
        copy.wait_recv()
    total = own_part[...]
    for d in offsets:
        total = total + backbuf[REACH + d].astype(F32)
    fgrad[...] = total.astype(BF16)
    put_fgrad = pltpu.make_async_copy(fgrad, fgrad_out, out_sem.at[1])
    put_fgrad.start()

    for step, copy in sorted(ygs, key=lambda pair: min(pair[0], NY - pair[0])):
        copy.wait_recv()
        pass_on((y + NY - step) % NY, step)
    put_wgrad = pltpu.make_async_copy(yg, wgrad_out.at[core], out_sem.at[2])
    put_wgrad.start()
    for copy in cgs:
        copy.wait()
    put_hidden.wait()
    put_fgrad.wait()
    put_wgrad.wait()
    for copy in list(halo.values()) + list(cots.values()) + list(aggs.values()) + [core_copy] + ys + hbs + xs + xgs:
        copy.wait_send()
    for _, copy in ygs:
        copy.wait_send()


def body(features, weight, cotangent, tile_val, tile_row, tile_col, tile_count):
    rows, panel = features.shape
    slots = tile_val.shape[1]
    reps = lax.axis_size("rep")
    nodes = rows * lax.axis_size("blk")
    f_in, hid = weight.shape
    wide = cotangent.shape[1]
    pieces = hid // TILE
    piece_rows = panel // 2
    x_rows = SUB * (-(-piece_rows // (SUB * NX)))
    group = ZL * NX
    vmem = pltpu.VMEM
    dma = pltpu.SemaphoreType.DMA
    scratch = [
        vmem((rows, panel), BF16),
        vmem((reps, 2 * TILE, hid), BF16),
        vmem((slots, TILE, TILE), BF16),
        vmem((WIDE, 3 * TILE, TILE), BF16),
        vmem((WIDE, rows, 2 * TILE), BF16),
        vmem((WIDE, TILE, 2 * rows), BF16),
        vmem((rows, TILE), F32),
        vmem((rows, TILE), F32),
        vmem((rows, TILE), F32),
        vmem((rows, TILE), F32),
        vmem((reps, 3 * TILE, TILE), BF16),
        vmem((panel, rows), BF16),
        vmem((reps, rows, wide), F32),
        vmem((reps, rows, wide), BF16),
        vmem((reps, rows, wide), BF16),
        vmem((rows, wide), BF16),
        vmem((rows, 2 * TILE), F32),
        vmem((rows, TILE), BF16),
        vmem((2 * rows, TILE), BF16),
        vmem((3 * TILE, TILE), F32),
        vmem((WIDE, 3 * TILE, TILE), BF16),
        vmem((WIDE, 3 * TILE, TILE), BF16),
        vmem((3 * TILE, TILE), BF16),
        vmem((pieces, piece_rows, TILE), BF16),
        vmem((pieces, piece_rows, TILE), BF16),
        vmem((pieces, piece_rows, TILE), F32),
        vmem((pieces, piece_rows, TILE), BF16),
        vmem((pieces, piece_rows, TILE), BF16),
        vmem((NX, x_rows, TILE), BF16),
        vmem((group, x_rows, TILE), BF16),
        vmem((NX, x_rows, TILE), BF16),
        vmem((pieces, piece_rows, TILE), BF16),
    ] + [
        dma((n,))
        for n in (
            3, 2 * reps, WIDE, WIDE, reps, reps, reps, reps, 1, 1,
            NY, NY, group, group, NX, NX, NY, NY, NY, NY, WIDE, WIDE, 3,
        )
    ]
    anywhere = pl.BlockSpec(memory_space=pl.ANY)
    scalar = pl.BlockSpec(memory_space=pltpu.SMEM)
    hidden, wgrad, fgrad = pl.pallas_call(
        functools.partial(kernel, nodes, slots, reps),
        out_shape=(
            jax.ShapeDtypeStruct((rows, wide), BF16),
            jax.ShapeDtypeStruct((2, pieces, piece_rows, TILE), BF16),
            jax.ShapeDtypeStruct((3 * TILE, TILE), BF16),
        ),
        in_specs=[anywhere] * 4 + [scalar] * 3,
        out_specs=(anywhere,) * 3,
        scratch_shapes=scratch,
        compiler_params=pltpu.CompilerParams(
            collective_id=0, has_side_effects=True, vmem_limit_bytes=48 * 1024 * 1024
        ),
    )(features, weight, cotangent, tile_val, tile_row, tile_col, tile_count)
    lanes = pieces // 2
    weight_grad = (
        wgrad.reshape(2, lanes, 2, piece_rows, TILE).transpose(2, 3, 0, 1, 4).reshape(panel, hid).astype(F32)
    )
    high = panel - TILE
    right = jnp.concatenate([fgrad[2 * TILE :, :high], fgrad[2 * TILE :, high:]], axis=0)
    feature_grad = jnp.concatenate([fgrad[: 2 * TILE], right], axis=1)
    return hidden, weight_grad, feature_grad


def solution(mesh):
    placed = (
        P("blk", "rep"),
        P(),
        P("blk", "rep"),
        P("blk", None, None, None),
        P("blk", None),
        P("blk", None),
        P("blk"),
    )
    return jax.shard_map(
        body,
        mesh=mesh,
        in_specs=placed,
        out_specs=(P("blk", "rep"), P("rep", None), P("blk", "rep")),
        check_vma=False,
    )
```

time: 2070 us -> 93.7 us (0.05)
  waiting for transfers between devices: 1930 us -> 0 us
  Pallas kernels: 0 us -> 83.1 us
  starting transfers between devices: 67.9 us -> 0 us
  blocking collectives: 37.8 us -> 0 us
    psum x1 -> x0, waiting for transfers between devices: 1900 us -> none  [body(): weight_grad = lax.psum(partial_grad, 'blk') / jnp.sqrt(jnp.float32(nodes))]
    pallas_call x0 -> x1, Pallas kernels: none -> 83.1 us  [body(): pl.pallas_call(functools.partial(kernel, nodes, slots, reps), out_shape=(...]
    ppermute x16 -> x0, starting transfers between devices: 67.8 us -> none  [passed_along(): return lax.ppermute(value, axis, pairs)]
    all_gather x2 -> x0, blocking collectives: 37.8 us -> none  [the longest x1 24.6 us: body(): lax.all_gather(cotangent, 'rep', axis=1, tiled=True)]
    ppermute x16 -> x0, waiting for transfers between devices: 24.4 us -> none  [passed_along(): return lax.ppermute(value, axis, pairs)]
  transfers between devices with their start and end apart: 17 -> 0, of which waited for: 5 -> 0; matrix products, arithmetic and copies ran while one was open for 1% -> 0% of each run, Pallas kernels for 0% -> 0%
where the time goes in v1:
time: 93.7 us; the launch traced here: 93.4 us
  Pallas kernels  83.1 us (89%)
  local copies, waits for them, and re-layouts  8.88 us (9%)
  between operations  1.33 us (1%)
    pallas_call x1, Pallas kernels, body(): pl.pallas_call(functools.partial(kernel, nodes, slots, reps), out_shape=(...  83.1 us
    unnamed x13, local copies, waits for them, and re-layouts  7.09 us

profile of v1, /device:TPU:1, one launch (start us, length us, event | category | flops | bytes accessed | tf_op | source)
XLA Modules:
  0.0 93.4 jit_solution(10165770639292408137)
XLA Ops:
  1.3 1.0 %copy.10.feat_hbm = bf16[256,192]{1,0:T(8,128)(2,1)S(1)} copy(bf16[256,192]{0,1:T(8,128)(2,1)} %param.7) | data formatting | bytes 196608 | tf_op args[0]
  2.3 0.0 copy-start
  2.3 1.4 %copy-done = bf16[768,1024]{1,0:T(8,128)(2,1)S(1)} copy-done((bf16[768,1024]{1,0:T(8,128)(2,1)S(1)}, bf16[768,1024]{1,0:T(8,128)(2,1)}, u32[]{:S(2)}) %copy-start) | copy-done | bytes 1572888
  3.7 0.0 copy-start.1
  3.7 1.1 %copy-done.1 = bf16[1,20,128,128]{3,2,1,0:T(8,128)(2,1)S(1)} copy-done((bf16[1,20,128,128]{3,2,1,0:T(8,128)(2,1)S(1)}, bf16[1,20,128,128]{3,2,1,0:T(8,128)(2,1)}, u32[]{:S(2)}) %copy-start.1) | copy-done | bytes 655384
  4.8 0.0 copy-start.2
  4.8 0.9 copy-done.2
  5.7 0.0 copy-start.3
  5.7 0.7 copy-done.3
  6.3 0.0 copy-start.4
  6.3 0.7 copy-done.4
  7.0 83.1 %shard_map.94 = (bf16[256,256]{1,0:T(8,128)(2,1)S(1)}, bf16[2,8,96,128]{3,2,1,0:T(8,128)(2,1)S(1)}, bf16[384,128]{1,0:T(8,128)(2,1)S(1)}) custom-call(bf16[256,192]{1,0:T(8,128)(2,1)S(1)} %copy.10.feat_hbm, bf16[768,1024]{1,0:T(8,128)(2,1)S(1)} %copy-done, bf16[256,256]{1,0:T(8,128)(2,1)S(1)} %copy-done.2, bf16[1,20,128,128]{3,2,1,0:T(8,128)(2,1)S(1)} %copy-done.1, ...), custom_call_target="tpu_custom_call" | custom-call | tf_op jit(solution)/shard_map/pallas_call | solution.py:446
  90.1 0.1 fusion
  90.2 0.7 copy.12
  91.0 0.1 convert_bitcast_fusion
  91.0 0.5 copy.11
  91.5 1.2 %reshape.12 = f32[192,1024]{1,0:T(8,128)} reshape(f32[2,96,2,4,128]{4,3,2,1,0:T(4,128)S(1)} %copy.11) | data formatting | bytes 1572864 | tf_op jit(solution)/shard_map/convert_element_type | solution.py:462
  92.7 0.7 copy.15
  (2 shorter events, 0.0 us)
Async XLA Ops:
  2.3 1.4 %copy-start = (bf16[768,1024]{1,0:T(8,128)(2,1)S(1)}, bf16[768,1024]{1,0:T(8,128)(2,1)}, u32[]{:S(2)}) copy-start(bf16[768,1024]{1,0:T(8,128)(2,1)} %weight_hbm.1) | copy-start | bytes 4718596
  3.7 1.1 %copy-start.1 = (bf16[1,20,128,128]{3,2,1,0:T(8,128)(2,1)S(1)}, bf16[1,20,128,128]{3,2,1,0:T(8,128)(2,1)}, u32[]{:S(2)}) copy-start(bf16[1,20,128,128]{3,2,1,0:T(8,128)(2,1)} %val_hbm.1) | copy-start | bytes 1966084
  4.8 0.9 copy-start.2
  5.7 0.7 copy-start.3
  6.3 0.7 copy-start.4

commit v2 on v1

v2 whole, which is shorter than its diff:
```python
import functools

import jax
import jax.numpy as jnp
from jax import lax
from jax.experimental import pallas as pl
from jax.experimental.pallas import tpu as pltpu
from jax.sharding import PartitionSpec as P

TILE = 128
ROWT = 2
REACH = 4
WIDE = 2 * REACH + 1
ZL, NY, NX, NC = 2, 8, 8, 2
SUB = 16
VMEM_BYTES = 60 * 1024 * 1024
F32 = jnp.float32
BF16 = jnp.bfloat16


def mm(a, b):
    return jnp.dot(a, b, preferred_element_type=F32)


def mm_nt(a, b):
    return lax.dot_general(a, b, (((1,), (1,)), ((), ())), preferred_element_type=F32)


def remote(src, dst, send, recv, where):
    return pltpu.make_async_remote_copy(
        src_ref=src, dst_ref=dst, send_sem=send, recv_sem=recv,
        device_id=where, device_id_type=pl.DeviceIdType.MESH,
    )


def kernel(
    nodes, slots, reps,
    feat_hbm, weight_hbm, cot_hbm, val_hbm, row_hbm, col_hbm, count_hbm,
    hidden_out, wgrad_out, fgrad_out,
    row_ref, col_ref, count_ref,
    weight, vals, win, chain, adj, scale, acc,
    aggbuf, pre, cotbuf, grad, hidden, back, own_part, parts, backbuf, fgrad,
    core_out, core_in, core_own, y_out, y_in, x_out, x_in, xg, yg,
    local_sem, halo_s, halo_r, pass_s, pass_r, cot_s, cot_r, agg_s, agg_r, core_s, core_r,
    y_s, y_r, x_s, x_r, xg_s, xg_r, yg_s, yg_r, cg_s, cg_r, hb_s, hb_r, out_sem,
):
    blk = lax.axis_index("blk")
    rep = lax.axis_index("rep")
    blocks = ZL * NY * NX * NC
    core = blk % NC
    x = (blk // NC) % NX
    y = (blk // (NC * NX)) % NY
    zl = blk // (NC * NX * NY)
    xz = zl * NX + x
    toward = 1 - 2 * core
    panel = win.shape[1]
    pieces, piece_rows, _ = core_out.shape
    x_rows = x_out.shape[1]

    def blk_at(offset):
        return {"blk": (blk + offset + blocks) % blocks}

    def y_at(step):
        return {"blk": ((zl * NY + (y + step) % NY) * NX + x) * NC + core}

    def x_at(step):
        return {"blk": ((zl * NY + y) * NX + (x + step) % NX) * NC + core}

    def xz_at(step):
        g = (xz + step) % (ZL * NX)
        return {"blk": (((g // NX) * NY + y) * NX + g % NX) * NC + core}

    def rep_at(step):
        return {"rep": (rep + step) % reps}

    sibling = {"blk": blk + toward}
    offsets = [d for d in range(-REACH, REACH + 1) if d != 0]

    get_feat = pltpu.make_async_copy(feat_hbm, win.at[REACH], local_sem.at[0])
    get_feat.start()
    get_cot = pltpu.make_async_copy(cot_hbm, cotbuf.at[rep], local_sem.at[1])
    get_cot.start()

    barrier = pltpu.get_barrier_semaphore()

    def greet(where):
        pl.semaphore_signal(barrier, inc=1, device_id=where, device_id_type=pl.DeviceIdType.MESH)

    for d in offsets:
        greet(blk_at(d))
    for step in range(1, reps):
        greet(rep_at(step))
    for step in range(1, NY):
        greet(y_at(step))
    for step in range(1, ZL * NX):
        greet(xz_at(step))
    greeted = len(offsets) + reps - 1 + NY - 1 + ZL * NX - 1

    get_rows = pltpu.make_async_copy(row_hbm, row_ref, local_sem.at[2])
    get_cols = pltpu.make_async_copy(col_hbm, col_ref, local_sem.at[3])
    get_count = pltpu.make_async_copy(count_hbm, count_ref, local_sem.at[4])
    get_vals = pltpu.make_async_copy(val_hbm.at[0], vals, local_sem.at[5])
    get_weight = pltpu.make_async_copy(weight_hbm, weight, local_sem.at[6])
    for copy in (get_rows, get_cols, get_count, get_vals, get_weight):
        copy.start()
    get_feat.wait()
    get_cot.wait()
    get_rows.wait()
    get_cols.wait()
    get_count.wait()

    count = count_ref[0]
    keys = [jnp.where(s < count, row_ref[0, s] * (WIDE * ROWT) + col_ref[0, s], -1 - s) for s in range(slots)]
    rows = [jnp.where(s < count, row_ref[0, s], -1) for s in range(slots)]
    chain[slots] = jnp.zeros((TILE, TILE), F32)

    pl.semaphore_wait(barrier, greeted)

    halo = {}
    for i, d in enumerate((-4 * toward, 2, -2, 4 * toward)):
        halo[i] = remote(win.at[REACH], win.at[REACH - d], halo_s.at[i], halo_r.at[i], blk_at(d))
        halo[i].start()
    to_sibling = [remote(win.at[REACH], win.at[REACH - toward], pass_s.at[3], pass_r.at[3], sibling)]
    to_sibling[0].start()
    cots = []

    def gather_rep(buf, send, recv, out):
        for i, step in enumerate((1, -1) if reps > 2 else (1,)):
            copy = remote(buf.at[rep], buf.at[rep], send.at[i], recv.at[i], rep_at(step + reps))
            copy.start()
            out.append(copy)

    def pass_rep(buf, send, recv, out):
        half = buf.shape[1] // 2
        for i, step in enumerate((1, -1)):
            out[i].wait_recv()
            owner = (rep - step + reps) % reps
            at = buf.at[owner, pl.ds(i * half, half)]
            copy = remote(at, at, send.at[2 + i], recv.at[2 + i], rep_at(step + reps))
            copy.start()
            out.append(copy)

    gather_rep(cotbuf, cot_s, cot_r, cots)

    get_vals.wait()
    chunk = 32

    def one_where(cond):
        return jnp.where(cond, 1.0, 0.0).astype(F32)

    for s in range(slots):
        before = jnp.int32(slots)
        for t in range(s):
            before = jnp.where(keys[t] == keys[s], t, before)
        v = vals[s].astype(F32)
        chain[s] = v + chain[before]

    @pl.loop(0, TILE // chunk)
    def _(c):
        at = pl.ds(pl.multiple_of(c * chunk, chunk), chunk)
        sums = [jnp.zeros((chunk, TILE), F32) for _ in range(ROWT)]
        for s in range(slots):
            v = vals[s, at, :].astype(F32)
            sq = v * v
            for r in range(ROWT):
                sums[r] = sums[r] + sq * one_where(rows[s] == r)
        for r in range(ROWT):
            acc[pl.ds(pl.multiple_of(c * chunk, chunk), chunk), r * TILE : (r + 1) * TILE] = sums[r]

    for r in range(ROWT):
        row_sq = jnp.sum(acc[0:TILE, r * TILE : (r + 1) * TILE].T, axis=0, keepdims=True)
        scale[:, r * TILE : (r + 1) * TILE] = jnp.broadcast_to(lax.rsqrt(1.0 + row_sq), (8, TILE))

    @pl.loop(0, WIDE)
    def _(j):
        for r in range(ROWT):
            for t in range(ROWT):
                last = jnp.int32(slots)
                for s in range(slots):
                    last = jnp.where(keys[s] == r * (WIDE * ROWT) + j * ROWT + t, s, last)
                adj[j, r * TILE : (r + 1) * TILE, t * TILE : (t + 1) * TILE] = chain[last].astype(BF16)

    acc[...] = mm_nt(win[REACH], adj[REACH])

    def add_block(j):
        acc[...] += mm_nt(win[j], adj[j])

    for i, d in enumerate((-4 * toward, 2, -2)):
        halo[i].wait_recv()
        copy = remote(win.at[REACH - d], win.at[REACH - d - toward], pass_s.at[i], pass_r.at[i], sibling)
        copy.start()
        to_sibling.append(copy)
    if reps > 2:
        pass_rep(cotbuf, cot_s, cot_r, cots)
    halo[3].wait_recv()
    for d in (-4, -2, 2, 4):
        add_block(REACH + d)
    for copy in to_sibling:
        copy.wait_recv()
    for d in (-3, -1, 1, 3):
        add_block(REACH + d)

    node_scale = scale[0:1, :]
    aggbuf[rep] = (win[REACH].astype(F32) + node_scale * acc[...]).astype(BF16)
    aggs = []
    gather_rep(aggbuf, agg_s, agg_r, aggs)

    get_weight.wait()
    groups = pre.shape[0]
    wide = pre.shape[2]

    def weight_rows(q):
        return pl.ds(pl.multiple_of(q * panel, 64), panel)

    def add_pre(q, first):
        lhs = aggbuf[q].astype(F32).T.astype(BF16)
        for n in range(groups):
            part = mm(lhs, weight[weight_rows(q), n * wide : (n + 1) * wide])
            if first:
                pre[n] = part
            else:
                pre[n] += part

    add_pre(rep, True)
    if reps > 2:
        pass_rep(aggbuf, agg_s, agg_r, aggs)
        add_pre((rep + reps - 1) % reps, False)
        add_pre((rep + 1) % reps, False)
        for copy in cots[2:] + aggs[2:]:
            copy.wait_recv()
        add_pre((rep + 2) % reps, False)
    else:
        cots[0].wait_recv()
        aggs[0].wait_recv()
        add_pre((rep + 1) % reps, False)

    def grad_at(n):
        v = pre[n]
        sig = jax.nn.sigmoid(v)
        slope = sig * (1.0 + v * (1.0 - sig))
        grad[n] = (cotbuf[n].astype(F32) * slope).astype(BF16)

    def weight_part(n, u, out):
        part = mm(aggbuf[rep], grad[n]).astype(out.dtype)
        for t in range(wide // TILE):
            for h in range(2):
                out[(u * (wide // TILE) + t) * 2 + h] = part[
                    h * piece_rows : (h + 1) * piece_rows, t * TILE : (t + 1) * TILE
                ]

    half = groups // 2
    for u in range(half):
        n = (1 - core) * half + u
        grad_at(n)
        weight_part(n, u, core_out)
    core_copy = remote(core_out, core_in, core_s.at[0], core_r.at[0], sibling)
    core_copy.start()
    for u in range(half):
        n = core * half + u
        grad_at(n)
        weight_part(n, u, core_own)

    back_sum = mm_nt(weight[weight_rows(rep), 0:wide], grad[0])
    for n in range(1, groups):
        back_sum = back_sum + mm_nt(weight[weight_rows(rep), n * wide : (n + 1) * wide], grad[n])
    back[...] = back_sum

    core_copy.wait_recv()
    for i in range(pieces):
        total = core_own[i] + core_in[i].astype(F32)
        core_own[i] = total
        y_out[i] = total.astype(BF16)
    ys = []
    for step in (4, 3, 5, 2, 6, 1, 7) if NY == 8 else range(1, NY):
        copy = remote(y_out.at[(y + step) % NY], y_in.at[y], y_s.at[step], y_r.at[step], y_at(step))
        copy.start()
        ys.append(copy)

    scaled = (node_scale * back[...]).astype(BF16)
    hbs = []
    for d in (4, -4, 3, -3, 2, -2, 1, -1):
        j = REACH + d
        parts[j] = mm(scaled, adj[j]).astype(BF16)
        copy = remote(parts.at[j], backbuf.at[REACH - d], hb_s.at[d + REACH], hb_r.at[REACH - d], blk_at(d))
        copy.start()
        hbs.append(copy)
    own_part[...] = mm(scaled, adj[REACH]) + back[...]

    v = pre[rep]
    hidden[...] = (v * jax.nn.sigmoid(v)).astype(BF16)
    put_hidden = pltpu.make_async_copy(hidden, hidden_out, out_sem.at[0])
    put_hidden.start()

    for copy in ys:
        copy.wait_recv()
    total = core_own[y]
    for step in range(1, NY):
        total = total + y_in[(y + step) % NY].astype(F32)
    filled = piece_rows // x_rows
    x_out[0:filled] = total.astype(BF16).reshape(filled, x_rows, TILE)
    if filled < NX:
        x_out[filled:NX] = jnp.zeros((NX - filled, x_rows, TILE), BF16)
    xs = []
    for step in range(1, ZL * NX):
        to = ((xz + step) % (ZL * NX)) % NX
        copy = remote(x_out.at[to], x_in.at[xz], x_s.at[step], x_r.at[step], xz_at(step))
        copy.start()
        xs.append(copy)
    x_in[xz] = x_out[x]
    for copy in xs:
        copy.wait_recv()
    total = x_in[0].astype(F32)
    for g in range(1, ZL * NX):
        total = total + x_in[g].astype(F32)
    xg[x] = (total * nodes ** -0.5).astype(BF16)
    xgs = []
    for step in range(1, NX):
        copy = remote(xg.at[x], xg.at[x], xg_s.at[step], xg_r.at[step], x_at(step))
        copy.start()
        xgs.append(copy)
    for copy in xgs:
        copy.wait_recv()
    yg[y] = xg[0:filled].reshape(piece_rows, TILE)
    ygs = []
    for step in (4, 3, 5, 2, 6, 1, 7) if NY == 8 else range(1, NY):
        copy = remote(yg.at[y], yg.at[y], yg_s.at[step], yg_r.at[step], y_at(step))
        copy.start()
        ygs.append((step, copy))
    cgs = []
    puts = []

    def place(i):
        lane = core * (pieces // 2 * TILE) + (i // 2) * TILE
        at = (
            pl.ds(pl.multiple_of((i % 2) * piece_rows, piece_rows), piece_rows),
            pl.ds(pl.multiple_of(lane, TILE), TILE),
        )
        return wgrad_out.at[at]

    def pass_on(at, step):
        copy = remote(yg.at[at], place(at), cg_s.at[step], cg_r.at[step], sibling)
        copy.start()
        cgs.append(copy)
        copy = pltpu.make_async_copy(yg.at[at], place(at), out_sem.at[2 + step])
        copy.start()
        puts.append(copy)

    pass_on(y, 0)

    for copy in hbs:
        copy.wait_recv()
    total = own_part[...]
    for d in offsets:
        total = total + backbuf[REACH + d].astype(F32)
    fgrad[...] = total.astype(BF16)
    put_fgrad = pltpu.make_async_copy(fgrad, fgrad_out, out_sem.at[1])
    put_fgrad.start()

    for step, copy in sorted(ygs, key=lambda pair: min(pair[0], NY - pair[0])):
        copy.wait_recv()
        pass_on((y + NY - step) % NY, step)
    for copy in cgs + puts:
        copy.wait()
    put_hidden.wait()
    put_fgrad.wait()
    for copy in list(halo.values()) + to_sibling + cots + aggs + [core_copy] + ys + hbs + xs + xgs:
        copy.wait_send()
    for _, copy in ygs:
        copy.wait_send()


def finish(hidden_in, wgrad_in, fgrad_in, hidden_out, wgrad_out, fgrad_out, sems):
    put_hidden = pltpu.make_async_copy(hidden_in, hidden_out, sems.at[0])
    put_hidden.start()
    put_fgrad = pltpu.make_async_copy(fgrad_in, fgrad_out, sems.at[1])
    put_fgrad.start()
    wgrad_out[...] = wgrad_in[...].astype(F32)
    put_hidden.wait()
    put_fgrad.wait()


def body(features, weight, cotangent, tile_val, tile_row, tile_col, tile_count):
    rows, panel = features.shape
    slots = tile_val.shape[1]
    reps = lax.axis_size("rep")
    nodes = rows * lax.axis_size("blk")
    f_in, hid = weight.shape
    wide = cotangent.shape[1]
    pieces = hid // TILE
    piece_rows = panel // 2
    x_rows = SUB * (-(-piece_rows // (SUB * NX)))
    group = ZL * NX
    vmem = pltpu.VMEM
    smem = pltpu.SMEM
    dma = pltpu.SemaphoreType.DMA
    scratch = [
        smem((1, slots), jnp.int32),
        smem((1, slots), jnp.int32),
        smem((1,), jnp.int32),
        vmem((f_in, hid), BF16),
        vmem((slots, TILE, TILE), BF16),
        vmem((WIDE, panel, rows), BF16),
        vmem((slots + 1, TILE, TILE), F32),
        vmem((WIDE, rows, rows), BF16),
        vmem((8, rows), F32),
        vmem((panel, rows), F32),
        vmem((reps, panel, rows), BF16),
        vmem((reps, rows, wide), F32),
        vmem((reps, rows, wide), BF16),
        vmem((reps, rows, wide), BF16),
        vmem((rows, wide), BF16),
        vmem((panel, rows), F32),
        vmem((panel, rows), F32),
        vmem((WIDE, panel, rows), BF16),
        vmem((WIDE, panel, rows), BF16),
        vmem((panel, rows), BF16),
        vmem((pieces, piece_rows, TILE), BF16),
        vmem((pieces, piece_rows, TILE), BF16),
        vmem((pieces, piece_rows, TILE), F32),
        vmem((pieces, piece_rows, TILE), BF16),
        vmem((pieces, piece_rows, TILE), BF16),
        vmem((NX, x_rows, TILE), BF16),
        vmem((group, x_rows, TILE), BF16),
        vmem((NX, x_rows, TILE), BF16),
        vmem((pieces, piece_rows, TILE), BF16),
    ] + [
        dma((n,))
        for n in (
            7, 4, 4, 4, 4, 4, 4, 4, 4, 1, 1,
            NY, NY, group, group, NX, NX, NY, NY, NY, NY, WIDE, WIDE, 2 + NY,
        )
    ]
    anywhere = pl.BlockSpec(memory_space=pl.ANY)
    hbm = pl.BlockSpec(memory_space=pltpu.HBM)
    whole = pl.BlockSpec(memory_space=pltpu.VMEM)
    results = pl.pallas_call(
        functools.partial(kernel, nodes, slots, reps),
        out_shape=(
            jax.ShapeDtypeStruct((rows, wide), BF16),
            jax.ShapeDtypeStruct((panel, hid), BF16),
            jax.ShapeDtypeStruct((panel, rows), BF16),
        ),
        in_specs=[hbm] * 7,
        out_specs=(anywhere,) * 3,
        scratch_shapes=scratch,
        compiler_params=pltpu.CompilerParams(
            collective_id=0, has_side_effects=True, vmem_limit_bytes=VMEM_BYTES
        ),
    )(features.T, weight, cotangent, tile_val, tile_row, tile_col, tile_count)
    hidden, weight_grad, feature_grad = pl.pallas_call(
        finish,
        out_shape=(
            jax.ShapeDtypeStruct((rows, wide), BF16),
            jax.ShapeDtypeStruct((panel, hid), F32),
            jax.ShapeDtypeStruct((panel, rows), BF16),
        ),
        in_specs=[anywhere, whole, anywhere],
        out_specs=(hbm, whole, hbm),
        scratch_shapes=[dma((2,))],
        compiler_params=pltpu.CompilerParams(vmem_limit_bytes=VMEM_BYTES),
    )(*results)
    return hidden, weight_grad, feature_grad.T


def solution(mesh):
    placed = (
        P("blk", "rep"),
        P(),
        P("blk", "rep"),
        P("blk", None, None, None),
        P("blk", None),
        P("blk", None),
        P("blk"),
    )
    return jax.shard_map(
        body,
        mesh=mesh,
        in_specs=placed,
        out_specs=(P("blk", "rep"), P("rep", None), P("blk", "rep")),
        check_vma=False,
    )
```

time: 93.7 us -> 89.9 us (0.959)
  local copies, waits for them, and re-layouts: 8.88 us -> 0 us
  Pallas kernels: 83.1 us -> 88.4 us
    pallas_call x0 -> x1, Pallas kernels: none -> 9.94 us  [body(): pl.pallas_call(finish, out_shape=(jax.ShapeDtypeStruct((rows, wide), BF16...]
    unnamed x13 -> x0, local copies, waits for them, and re-layouts: 7.09 us -> none
    pallas_call x1, Pallas kernels: 83.1 us -> 78.4 us  [body(): pl.pallas_call(functools.partial(kernel, nodes, slots, reps), out_shape=(...]
    convert_element_type x2 -> x0, local copies, waits for them, and re-layouts: 1.7 us -> none  [body(): wgrad.reshape(2, lanes, 2, piece_rows, TILE).transpose(2, 3, 0, 1, 4)]
where the time goes in v2:
time: 89.9 us; the launch traced here: 89.6 us
  Pallas kernels  88.4 us (98%)
  between operations  1.29 us (1%)
    pallas_call x1, Pallas kernels, body(): pl.pallas_call(functools.partial(kernel, nodes, slots, reps), out_shape=(...  78.4 us
    pallas_call x1, Pallas kernels, body(): pl.pallas_call(finish, out_shape=(jax.ShapeDtypeStruct((rows, wide), BF16...  9.94 us

profile of v2, /device:TPU:1, one launch (start us, length us, event | category | flops | bytes accessed | tf_op | source)
XLA Modules:
  0.0 89.6 jit_solution(1341536093927212559)
XLA Ops:
  1.3 78.4 %shard_map.94 = (bf16[256,256]{1,0:T(8,128)(2,1)}, bf16[192,1024]{1,0:T(8,128)(2,1)}, bf16[192,256]{1,0:T(8,128)(2,1)}) custom-call(bf16[192,256]{1,0:T(8,128)(2,1)} %bitcast.2, bf16[768,1024]{1,0:T(8,128)(2,1)} %weight_hbm.1, bf16[256,256]{1,0:T(8,128)(2,1)} %cot_hbm.1, bf16[1,20,128,128]{3,2,1,0:T(8,128)(2,1)} %val_hbm.1, s32[1,20]{1,0:T(1,128)} %row_hbm.1, ...), custom_call_target="tpu_custom_call" | custom-call | tf_op jit(solution)/shard_map/pallas_call | solution.py:436
  79.7 9.9 %shard_map.95 = (bf16[256,256]{1,0:T(8,128)(2,1)}, f32[192,1024]{1,0:T(8,128)}, bf16[192,256]{1,0:T(8,128)(2,1)}) custom-call(bf16[256,256]{1,0:T(8,128)(2,1)} %get-tuple-element.9.hidden_in, bf16[192,1024]{1,0:T(8,128)(2,1)} %get-tuple-element.10.wgrad_in, bf16[192,256]{1,0:T(8,128)(2,1)} %get-tuple-element.11.fgrad_in), custom_call_target="tpu_custom_call" | custom-call | tf_op jit(solution)/shard_map/pallas_call | solution.py:450

commit v3 on v2

--- a/solution.py
+++ b/solution.py
@@ -39,10 +39,10 @@
     hidden_out, wgrad_out, fgrad_out,
     row_ref, col_ref, count_ref,
     weight, vals, win, chain, adj, scale, acc,
-    aggbuf, pre, cotbuf, grad, hidden, back, own_part, parts, backbuf, fgrad,
+    aggbuf, pre, cotbuf, grad, hidden, back, own_part, parts, sibbuf, backbuf, fgrad,
     core_out, core_in, core_own, y_out, y_in, x_out, x_in, xg, yg,
     local_sem, halo_s, halo_r, pass_s, pass_r, cot_s, cot_r, agg_s, agg_r, core_s, core_r,
-    y_s, y_r, x_s, x_r, xg_s, xg_r, yg_s, yg_r, cg_s, cg_r, hb_s, hb_r, out_sem,
+    y_s, y_r, x_s, x_r, xg_s, xg_r, yg_s, yg_r, cg_s, cg_r, hs_s, hs_r, hb_s, hb_r, out_sem,
 ):
     blk = lax.axis_index("blk")
     rep = lax.axis_index("rep")
@@ -74,7 +74,7 @@
         return {"rep": (rep + step) % reps}
 
     sibling = {"blk": blk + toward}
-    offsets = [d for d in range(-REACH, REACH + 1) if d != 0]
+    greet_at = [blk_at(d) for d in (-4, -2, 2, 4)] + [sibling]
 
     get_feat = pltpu.make_async_copy(feat_hbm, win.at[REACH], local_sem.at[0])
     get_feat.start()
@@ -86,15 +86,15 @@
     def greet(where):
         pl.semaphore_signal(barrier, inc=1, device_id=where, device_id_type=pl.DeviceIdType.MESH)
 
-    for d in offsets:
-        greet(blk_at(d))
+    for where in greet_at:
+        greet(where)
     for step in range(1, reps):
         greet(rep_at(step))
     for step in range(1, NY):
         greet(y_at(step))
     for step in range(1, ZL * NX):
         greet(xz_at(step))
-    greeted = len(offsets) + reps - 1 + NY - 1 + ZL * NX - 1
+    greeted = len(greet_at) + reps - 1 + NY - 1 + ZL * NX - 1
 
     get_rows = pltpu.make_async_copy(row_hbm, row_ref, local_sem.at[2])
     get_cols = pltpu.make_async_copy(col_hbm, col_ref, local_sem.at[3])
@@ -116,31 +116,26 @@
 
     pl.semaphore_wait(barrier, greeted)
 
-    halo = {}
-    for i, d in enumerate((-4 * toward, 2, -2, 4 * toward)):
-        halo[i] = remote(win.at[REACH], win.at[REACH - d], halo_s.at[i], halo_r.at[i], blk_at(d))
-        halo[i].start()
-    to_sibling = [remote(win.at[REACH], win.at[REACH - toward], pass_s.at[3], pass_r.at[3], sibling)]
-    to_sibling[0].start()
+    rows_half = panel // 2
+    parts_of = [pl.ds(h * rows_half, rows_half) for h in range(2)]
+    near = (-4 * toward, 2, -2, 4 * toward)
+    halo = [[], []]
+    to_sibling = [[], []]
+    for h in range(2):
+        own = win.at[REACH, parts_of[h]]
+        for i, d in enumerate(near):
+            copy = remote(own, win.at[REACH - d, parts_of[h]], halo_s.at[4 * h + i], halo_r.at[4 * h + i], blk_at(d))
+            copy.start()
+            halo[h].append(copy)
+        copy = remote(own, win.at[REACH - toward, parts_of[h]], pass_s.at[4 * h + 3], pass_r.at[4 * h + 3], sibling)
+        copy.start()
+        to_sibling[h].append(copy)
+
     cots = []
-
-    def gather_rep(buf, send, recv, out):
-        for i, step in enumerate((1, -1) if reps > 2 else (1,)):
-            copy = remote(buf.at[rep], buf.at[rep], send.at[i], recv.at[i], rep_at(step + reps))
-            copy.start()
-            out.append(copy)
-
-    def pass_rep(buf, send, recv, out):
-        half = buf.shape[1] // 2
-        for i, step in enumerate((1, -1)):
-            out[i].wait_recv()
-            owner = (rep - step + reps) % reps
-            at = buf.at[owner, pl.ds(i * half, half)]
-            copy = remote(at, at, send.at[2 + i], recv.at[2 + i], rep_at(step + reps))
-            copy.start()
-            out.append(copy)
-
-    gather_rep(cotbuf, cot_s, cot_r, cots)
+    for i, step in enumerate((1, -1)):
+        copy = remote(cotbuf.at[rep], cotbuf.at[rep], cot_s.at[i], cot_r.at[i], rep_at(step + reps))
+        copy.start()
+        cots.append(copy)
 
     get_vals.wait()
     chunk = 32
@@ -180,31 +175,50 @@
                     last = jnp.where(keys[s] == r * (WIDE * ROWT) + j * ROWT + t, s, last)
                 adj[j, r * TILE : (r + 1) * TILE, t * TILE : (t + 1) * TILE] = chain[last].astype(BF16)
 
-    acc[...] = mm_nt(win[REACH], adj[REACH])
-
-    def add_block(j):
-        acc[...] += mm_nt(win[j], adj[j])
-
-    for i, d in enumerate((-4 * toward, 2, -2)):
-        halo[i].wait_recv()
-        copy = remote(win.at[REACH - d], win.at[REACH - d - toward], pass_s.at[i], pass_r.at[i], sibling)
-        copy.start()
-        to_sibling.append(copy)
-    if reps > 2:
-        pass_rep(cotbuf, cot_s, cot_r, cots)
-    halo[3].wait_recv()
-    for d in (-4, -2, 2, 4):
-        add_block(REACH + d)
-    for copy in to_sibling:
-        copy.wait_recv()
-    for d in (-3, -1, 1, 3):
-        add_block(REACH + d)
-
     node_scale = scale[0:1, :]
-    aggbuf[rep] = (win[REACH].astype(F32) + node_scale * acc[...]).astype(BF16)
-    aggs = []
-    gather_rep(aggbuf, agg_s, agg_r, aggs)
-
+    aggs = [[], []]
+    for h in range(2):
+        total = mm_nt(win[REACH, parts_of[h], :], adj[REACH])
+        for i, d in enumerate(near[:3]):
+            halo[h][i].wait_recv()
+            copy = remote(
+                win.at[REACH - d, parts_of[h]], win.at[REACH - d - toward, parts_of[h]],
+                pass_s.at[4 * h + i], pass_r.at[4 * h + i], sibling,
+            )
+            copy.start()
+            to_sibling[h].append(copy)
+        halo[h][3].wait_recv()
+        for d in (-4, -2, 2, 4):
+            total = total + mm_nt(win[REACH + d, parts_of[h], :], adj[REACH + d])
+        for copy in to_sibling[h]:
+            copy.wait_recv()
+        for d in (-3, -1, 1, 3):
+            total = total + mm_nt(win[REACH + d, parts_of[h], :], adj[REACH + d])
+        aggbuf[rep, parts_of[h], :] = (win[REACH, parts_of[h], :].astype(F32) + node_scale * total).astype(BF16)
+        for i, step in enumerate((1, -1)):
+            at = aggbuf.at[rep, parts_of[h]]
+            copy = remote(at, at, agg_s.at[2 * h + i], agg_r.at[2 * h + i], rep_at(step + reps))
+            copy.start()
+            aggs[h].append(copy)
+        if h == 0:
+            half = cotbuf.shape[1] // 2
+            for i, step in enumerate((1, -1)):
+                cots[i].wait_recv()
+                at = cotbuf.at[(rep - step + reps) % reps, pl.ds(i * half, half)]
+                copy = remote(at, at, cot_s.at[2 + i], cot_r.at[2 + i], rep_at(step + reps))
+                copy.start()
+                cots.append(copy)
+
+    relays = []
+
+    def relay(i, step):
+        aggs[i][i].wait_recv()
+        at = aggbuf.at[(rep - step + reps) % reps, parts_of[i]]
+        copy = remote(at, at, agg_s.at[4 + i], agg_r.at[4 + i], rep_at(step + reps))
+        copy.start()
+        relays.append(copy)
+
+    relay(0, 1)
     get_weight.wait()
     groups = pre.shape[0]
     wide = pre.shape[2]
@@ -222,17 +236,14 @@
                 pre[n] += part
 
     add_pre(rep, True)
-    if reps > 2:
-        pass_rep(aggbuf, agg_s, agg_r, aggs)
-        add_pre((rep + reps - 1) % reps, False)
-        add_pre((rep + 1) % reps, False)
-        for copy in cots[2:] + aggs[2:]:
-            copy.wait_recv()
-        add_pre((rep + 2) % reps, False)
-    else:
-        cots[0].wait_recv()
-        aggs[0].wait_recv()
-        add_pre((rep + 1) % reps, False)
+    relay(1, -1)
+    aggs[1][0].wait_recv()
+    add_pre((rep + reps - 1) % reps, False)
+    aggs[0][1].wait_recv()
+    add_pre((rep + 1) % reps, False)
+    for copy in cots[2:] + relays:
+        copy.wait_recv()
+    add_pre((rep + 2) % reps, False)
 
     def grad_at(n):
         v = pre[n]
@@ -278,12 +289,27 @@
 
     scaled = (node_scale * back[...]).astype(BF16)
     hbs = []
-    for d in (4, -4, 3, -3, 2, -2, 1, -1):
-        j = REACH + d
+    hss = []
+    for i, d in enumerate((2, -2, -4 * toward)):
+        j = REACH + d + toward
         parts[j] = mm(scaled, adj[j]).astype(BF16)
-        copy = remote(parts.at[j], backbuf.at[REACH - d], hb_s.at[d + REACH], hb_r.at[REACH - d], blk_at(d))
+        copy = remote(parts.at[j], sibbuf.at[i], hs_s.at[i], hs_r.at[i], sibling)
+        copy.start()
+        hss.append(copy)
+
+    def send_back(i, d, where):
+        copy = remote(parts.at[REACH + d], backbuf.at[i], hb_s.at[i], hb_r.at[i], where)
         copy.start()
         hbs.append(copy)
+
+    for i, d, where in ((3, -4 * toward, blk_at(-4 * toward)), (4, toward, sibling)):
+        parts[REACH + d] = mm(scaled, adj[REACH + d]).astype(BF16)
+        send_back(i, d, where)
+    for i, d in enumerate((2, -2, 4 * toward)):
+        mine = mm(scaled, adj[REACH + d])
+        hss[i].wait_recv()
+        parts[REACH + d] = (mine + sibbuf[i].astype(F32)).astype(BF16)
+        send_back(i, d, blk_at(d))
     own_part[...] = mm(scaled, adj[REACH]) + back[...]
 
     v = pre[rep]
@@ -350,8 +376,8 @@
     for copy in hbs:
         copy.wait_recv()
     total = own_part[...]
-    for d in offsets:
-        total = total + backbuf[REACH + d].astype(F32)
+    for i in range(5):
+        total = total + backbuf[i].astype(F32)
     fgrad[...] = total.astype(BF16)
     put_fgrad = pltpu.make_async_copy(fgrad, fgrad_out, out_sem.at[1])
     put_fgrad.start()
@@ -363,20 +389,17 @@
         copy.wait()
     put_hidden.wait()
     put_fgrad.wait()
-    for copy in list(halo.values()) + to_sibling + cots + aggs + [core_copy] + ys + hbs + xs + xgs:
+    gathers = halo[0] + halo[1] + to_sibling[0] + to_sibling[1] + cots + aggs[0] + aggs[1] + relays
+    for copy in gathers + [core_copy] + ys + hss + hbs + xs + xgs:
         copy.wait_send()
     for _, copy in ygs:
         copy.wait_send()
 
 
-def finish(hidden_in, wgrad_in, fgrad_in, hidden_out, wgrad_out, fgrad_out, sems):
-    put_hidden = pltpu.make_async_copy(hidden_in, hidden_out, sems.at[0])
-    put_hidden.start()
-    put_fgrad = pltpu.make_async_copy(fgrad_in, fgrad_out, sems.at[1])
-    put_fgrad.start()
+def finish(hidden_in, wgrad_in, fgrad_in, hidden_out, wgrad_out, fgrad_out):
+    hidden_out[...] = hidden_in[...]
+    fgrad_out[...] = fgrad_in[...]
     wgrad_out[...] = wgrad_in[...].astype(F32)
-    put_hidden.wait()
-    put_fgrad.wait()
 
 
 def body(features, weight, cotangent, tile_val, tile_row, tile_col, tile_count):
@@ -403,7 +426,7 @@
         vmem((slots + 1, TILE, TILE), F32),
         vmem((WIDE, rows, rows), BF16),
         vmem((8, rows), F32),
-        vmem((panel, rows), F32),
+        vmem((TILE, rows), F32),
         vmem((reps, panel, rows), BF16),
         vmem((reps, rows, wide), F32),
         vmem((reps, rows, wide), BF16),
@@ -412,7 +435,8 @@
         vmem((panel, rows), F32),
         vmem((panel, rows), F32),
         vmem((WIDE, panel, rows), BF16),
-        vmem((WIDE, panel, rows), BF16),
+        vmem((3, panel, rows), BF16),
+        vmem((5, panel, rows), BF16),
         vmem((panel, rows), BF16),
         vmem((pieces, piece_rows, TILE), BF16),
         vmem((pieces, piece_rows, TILE), BF16),
@@ -426,8 +450,8 @@
     ] + [
         dma((n,))
         for n in (
-            7, 4, 4, 4, 4, 4, 4, 4, 4, 1, 1,
-            NY, NY, group, group, NX, NX, NY, NY, NY, NY, WIDE, WIDE, 2 + NY,
+            7, 8, 8, 8, 8, 4, 4, 6, 6, 1, 1,
+            NY, NY, group, group, NX, NX, NY, NY, NY, NY, 3, 3, 5, 5, 2 + NY,
         )
     ]
     anywhere = pl.BlockSpec(memory_space=pl.ANY)
@@ -454,9 +478,8 @@
             jax.ShapeDtypeStruct((panel, hid), F32),
             jax.ShapeDtypeStruct((panel, rows), BF16),
         ),
-        in_specs=[anywhere, whole, anywhere],
-        out_specs=(hbm, whole, hbm),
-        scratch_shapes=[dma((2,))],
+        in_specs=[whole] * 3,
+        out_specs=(whole,) * 3,
         compiler_params=pltpu.CompilerParams(vmem_limit_bytes=VMEM_BYTES),
     )(*results)
     return hidden, weight_grad, feature_grad.T

time: 89.9 us -> 78 us (0.87)
  Pallas kernels: 88.4 us -> 76.5 us
    pallas_call x1, Pallas kernels: 9.94 us -> 2.07 us  [body(): pl.pallas_call(finish, out_shape=(jax.ShapeDtypeStruct((rows, wide), BF16...]
    pallas_call x1, Pallas kernels: 78.4 us -> 74.4 us  [body(): pl.pallas_call(functools.partial(kernel, nodes, slots, reps), out_shape=(...]
where the time goes in v3:
time: 78 us; the launch traced here: 77.8 us
  Pallas kernels  76.5 us (98%)
  between operations  1.29 us (2%)
    pallas_call x1, Pallas kernels, body(): pl.pallas_call(functools.partial(kernel, nodes, slots, reps), out_shape=(...  74.4 us
    pallas_call x1, Pallas kernels, body(): pl.pallas_call(finish, out_shape=(jax.ShapeDtypeStruct((rows, wide), BF16...  2.07 us

profile of v3, /device:TPU:1, one launch (start us, length us, event | category | flops | bytes accessed | tf_op | source)
XLA Modules:
  0.0 77.8 jit_solution(2160760472031580445)
XLA Ops:
  1.3 74.4 %shard_map.94 = (bf16[256,256]{1,0:T(8,128)(2,1)}, bf16[192,1024]{1,0:T(8,128)(2,1)}, bf16[192,256]{1,0:T(8,128)(2,1)}) custom-call(bf16[192,256]{1,0:T(8,128)(2,1)} %bitcast.2, bf16[768,1024]{1,0:T(8,128)(2,1)} %weight_hbm.1, bf16[256,256]{1,0:T(8,128)(2,1)} %cot_hbm.1, bf16[1,20,128,128]{3,2,1,0:T(8,128)(2,1)} %val_hbm.1, s32[1,20]{1,0:T(1,128)} %row_hbm.1, ...), custom_call_target="tpu_custom_call" | custom-call | tf_op jit(solution)/shard_map/pallas_call | solution.py:460
  75.7 2.1 %shard_map.95 = (bf16[256,256]{1,0:T(8,128)(2,1)}, f32[192,1024]{1,0:T(8,128)}, bf16[192,256]{1,0:T(8,128)(2,1)}) custom-call(bf16[256,256]{1,0:T(8,128)(2,1)} %get-tuple-element.9.hidden_in, bf16[192,1024]{1,0:T(8,128)(2,1)} %get-tuple-element.10.wgrad_in, bf16[192,256]{1,0:T(8,128)(2,1)} %get-tuple-element.11.fgrad_in), custom_call_target="tpu_custom_call" | custom-call | tf_op jit(solution)/shard_map/pallas_call | solution.py:474

commit v4 on v3

--- a/solution.py
+++ b/solution.py
@@ -39,7 +39,7 @@
     hidden_out, wgrad_out, fgrad_out,
     row_ref, col_ref, count_ref,
     weight, vals, win, chain, adj, scale, acc,
-    aggbuf, pre, cotbuf, grad, hidden, back, own_part, parts, sibbuf, backbuf, fgrad,
+    aggbuf, pre, cotbuf, grad, hidden, back, own_part, parts, sibbuf, outbuf, backbuf, fgrad,
     core_out, core_in, core_own, y_out, y_in, x_out, x_in, xg, yg,
     local_sem, halo_s, halo_r, pass_s, pass_r, cot_s, cot_r, agg_s, agg_r, core_s, core_r,
     y_s, y_r, x_s, x_r, xg_s, xg_r, yg_s, yg_r, cg_s, cg_r, hs_s, hs_r, hb_s, hb_r, out_sem,
@@ -88,13 +88,13 @@
 
     for where in greet_at:
         greet(where)
-    for step in range(1, reps):
-        greet(rep_at(step))
+    for step in (1, -1):
+        greet(rep_at(step + reps))
     for step in range(1, NY):
         greet(y_at(step))
     for step in range(1, ZL * NX):
         greet(xz_at(step))
-    greeted = len(greet_at) + reps - 1 + NY - 1 + ZL * NX - 1
+    greeted = len(greet_at) + 2 + NY - 1 + ZL * NX - 1
 
     get_rows = pltpu.make_async_copy(row_hbm, row_ref, local_sem.at[2])
     get_cols = pltpu.make_async_copy(col_hbm, col_ref, local_sem.at[3])
@@ -260,56 +260,57 @@
                 ]
 
     half = groups // 2
+    share = pieces // half
+    core_copies = []
     for u in range(half):
         n = (1 - core) * half + u
         grad_at(n)
         weight_part(n, u, core_out)
-    core_copy = remote(core_out, core_in, core_s.at[0], core_r.at[0], sibling)
-    core_copy.start()
+        at = pl.ds(u * share, share)
+        copy = remote(core_out.at[at], core_in.at[at], core_s.at[u], core_r.at[u], sibling)
+        copy.start()
+        core_copies.append(copy)
     for u in range(half):
         n = core * half + u
         grad_at(n)
         weight_part(n, u, core_own)
 
+    def to_y(i):
+        where = {"blk": ((zl * NY + i) * NX + x) * NC + core}
+        return remote(y_out.at[i], y_in.at[y], y_s.at[i], y_r.at[y], where)
+
+    for u in range(half):
+        core_copies[u].wait_recv()
+        for i in range(u * share, (u + 1) * share):
+            total = core_own[i] + core_in[i].astype(F32)
+            core_own[i] = total
+            y_out[i] = total.astype(BF16)
+
+            @pl.when(y != i)
+            def _(i=i):
+                to_y(i).start()
+
     back_sum = mm_nt(weight[weight_rows(rep), 0:wide], grad[0])
     for n in range(1, groups):
         back_sum = back_sum + mm_nt(weight[weight_rows(rep), n * wide : (n + 1) * wide], grad[n])
     back[...] = back_sum
 
-    core_copy.wait_recv()
-    for i in range(pieces):
-        total = core_own[i] + core_in[i].astype(F32)
-        core_own[i] = total
-        y_out[i] = total.astype(BF16)
-    ys = []
-    for step in (4, 3, 5, 2, 6, 1, 7) if NY == 8 else range(1, NY):
-        copy = remote(y_out.at[(y + step) % NY], y_in.at[y], y_s.at[step], y_r.at[step], y_at(step))
-        copy.start()
-        ys.append(copy)
-
     scaled = (node_scale * back[...]).astype(BF16)
-    hbs = []
     hss = []
     for i, d in enumerate((2, -2, -4 * toward)):
         j = REACH + d + toward
-        parts[j] = mm(scaled, adj[j]).astype(BF16)
-        copy = remote(parts.at[j], sibbuf.at[i], hs_s.at[i], hs_r.at[i], sibling)
+        parts[i] = mm(scaled, adj[j]).astype(BF16)
+        copy = remote(parts.at[i], sibbuf.at[i], hs_s.at[i], hs_r.at[i], sibling)
         copy.start()
         hss.append(copy)
 
-    def send_back(i, d, where):
-        copy = remote(parts.at[REACH + d], backbuf.at[i], hb_s.at[i], hb_r.at[i], where)
-        copy.start()
-        hbs.append(copy)
-
-    for i, d, where in ((3, -4 * toward, blk_at(-4 * toward)), (4, toward, sibling)):
-        parts[REACH + d] = mm(scaled, adj[REACH + d]).astype(BF16)
-        send_back(i, d, where)
-    for i, d in enumerate((2, -2, 4 * toward)):
+    hb_list = ((3, -4 * toward), (4, toward), (0, 2), (1, -2), (2, 4 * toward))
+    for i, d in hb_list:
         mine = mm(scaled, adj[REACH + d])
-        hss[i].wait_recv()
-        parts[REACH + d] = (mine + sibbuf[i].astype(F32)).astype(BF16)
-        send_back(i, d, blk_at(d))
+        if i < 3:
+            hss[i].wait_recv()
+            mine = mine + sibbuf[i].astype(F32)
+        outbuf[i] = mine.astype(BF16)
     own_part[...] = mm(scaled, adj[REACH]) + back[...]
 
     v = pre[rep]
@@ -317,9 +318,10 @@
     put_hidden = pltpu.make_async_copy(hidden, hidden_out, out_sem.at[0])
     put_hidden.start()
 
-    for copy in ys:
-        copy.wait_recv()
     total = core_own[y]
+    for step in range(1, NY):
+        source = (y + step) % NY
+        remote(y_out.at[source], y_in.at[source], y_s.at[source], y_r.at[source], y_at(step)).wait_recv()
     for step in range(1, NY):
         total = total + y_in[(y + step) % NY].astype(F32)
     filled = piece_rows // x_rows
@@ -344,6 +346,11 @@
         copy = remote(xg.at[x], xg.at[x], xg_s.at[step], xg_r.at[step], x_at(step))
         copy.start()
         xgs.append(copy)
+    hbs = []
+    for i, d in hb_list:
+        copy = remote(outbuf.at[i], backbuf.at[i], hb_s.at[i], hb_r.at[i], sibling if i == 4 else blk_at(d))
+        copy.start()
+        hbs.append(copy)
     for copy in xgs:
         copy.wait_recv()
     yg[y] = xg[0:filled].reshape(piece_rows, TILE)
@@ -372,6 +379,10 @@
         puts.append(copy)
 
     pass_on(y, 0)
+
+    for step, copy in sorted(ygs, key=lambda pair: min(pair[0], NY - pair[0])):
+        copy.wait_recv()
+        pass_on((y + NY - step) % NY, step)
 
     for copy in hbs:
         copy.wait_recv()
@@ -382,15 +393,18 @@
     put_fgrad = pltpu.make_async_copy(fgrad, fgrad_out, out_sem.at[1])
     put_fgrad.start()
 
-    for step, copy in sorted(ygs, key=lambda pair: min(pair[0], NY - pair[0])):
-        copy.wait_recv()
-        pass_on((y + NY - step) % NY, step)
     for copy in cgs + puts:
         copy.wait()
     put_hidden.wait()
     put_fgrad.wait()
     gathers = halo[0] + halo[1] + to_sibling[0] + to_sibling[1] + cots + aggs[0] + aggs[1] + relays
-    for copy in gathers + [core_copy] + ys + hss + hbs + xs + xgs:
+    for i in range(NY):
+
+        @pl.when(y != i)
+        def _(i=i):
+            to_y(i).wait_send()
+
+    for copy in gathers + core_copies + hss + hbs + xs + xgs:
         copy.wait_send()
     for _, copy in ygs:
         copy.wait_send()
@@ -434,8 +448,9 @@
         vmem((rows, wide), BF16),
         vmem((panel, rows), F32),
         vmem((panel, rows), F32),
-        vmem((WIDE, panel, rows), BF16),
         vmem((3, panel, rows), BF16),
+        vmem((3, panel, rows), BF16),
+        vmem((5, panel, rows), BF16),
         vmem((5, panel, rows), BF16),
         vmem((panel, rows), BF16),
         vmem((pieces, piece_rows, TILE), BF16),
@@ -450,7 +465,7 @@
     ] + [
         dma((n,))
         for n in (
-            7, 8, 8, 8, 8, 4, 4, 6, 6, 1, 1,
+            7, 8, 8, 8, 8, 4, 4, 6, 6, 2, 2,
             NY, NY, group, group, NX, NX, NY, NY, NY, NY, 3, 3, 5, 5, 2 + NY,
         )
     ]

time: 78 us -> 78.4 us (level)
  no operation moved by 1% of the time
where the time goes in v4:
time: 78.4 us; the launch traced here: 78.2 us
  Pallas kernels  76.9 us (98%)
  between operations  1.29 us (2%)
    pallas_call x1, Pallas kernels, body(): pl.pallas_call(functools.partial(kernel, nodes, slots, reps), out_shape=(...  74.8 us
    pallas_call x1, Pallas kernels, body(): pl.pallas_call(finish, out_shape=(jax.ShapeDtypeStruct((rows, wide), BF16...  2.07 us

profile of v4, /device:TPU:1, one launch (start us, length us, event | category | flops | bytes accessed | tf_op | source)
XLA Modules:
  0.0 78.2 jit_solution(10285955312237463035)
XLA Ops:
  1.3 74.8 %shard_map.94 = (bf16[256,256]{1,0:T(8,128)(2,1)}, bf16[192,1024]{1,0:T(8,128)(2,1)}, bf16[192,256]{1,0:T(8,128)(2,1)}) custom-call(bf16[192,256]{1,0:T(8,128)(2,1)} %bitcast.2, bf16[768,1024]{1,0:T(8,128)(2,1)} %weight_hbm.1, bf16[256,256]{1,0:T(8,128)(2,1)} %cot_hbm.1, bf16[1,20,128,128]{3,2,1,0:T(8,128)(2,1)} %val_hbm.1, s32[1,20]{1,0:T(1,128)} %row_hbm.1, ...), custom_call_target="tpu_custom_call" | custom-call | tf_op jit(solution)/shard_map/pallas_call | solution.py:475
  76.1 2.1 %shard_map.95 = (bf16[256,256]{1,0:T(8,128)(2,1)}, f32[192,1024]{1,0:T(8,128)}, bf16[192,256]{1,0:T(8,128)(2,1)}) custom-call(bf16[256,256]{1,0:T(8,128)(2,1)} %get-tuple-element.9.hidden_in, bf16[192,1024]{1,0:T(8,128)(2,1)} %get-tuple-element.10.wgrad_in, bf16[192,256]{1,0:T(8,128)(2,1)} %get-tuple-element.11.fgrad_in), custom_call_target="tpu_custom_call" | custom-call | tf_op jit(solution)/shard_map/pallas_call | solution.py:489

commit v5 on v4

--- a/solution.py
+++ b/solution.py
@@ -179,7 +179,8 @@
     aggs = [[], []]
     for h in range(2):
         total = mm_nt(win[REACH, parts_of[h], :], adj[REACH])
-        for i, d in enumerate(near[:3]):
+        for i in (1, 2, 0):
+            d = near[i]
             halo[h][i].wait_recv()
             copy = remote(
                 win.at[REACH - d, parts_of[h]], win.at[REACH - d - toward, parts_of[h]],
@@ -243,10 +244,12 @@
     add_pre((rep + 1) % reps, False)
     for copy in cots[2:] + relays:
         copy.wait_recv()
-    add_pre((rep + 2) % reps, False)
+    last = (rep + 2) % reps
+    last_lhs = aggbuf[last].astype(F32).T.astype(BF16)
 
     def grad_at(n):
-        v = pre[n]
+        v = pre[n] + mm(last_lhs, weight[weight_rows(last), pl.ds(pl.multiple_of(n * wide, wide), wide)])
+        pre[n] = v
         sig = jax.nn.sigmoid(v)
         slope = sig * (1.0 + v * (1.0 - sig))
         grad[n] = (cotbuf[n].astype(F32) * slope).astype(BF16)
@@ -335,6 +338,11 @@
         copy.start()
         xs.append(copy)
     x_in[xz] = x_out[x]
+    hbs = []
+    for i, d in hb_list:
+        copy = remote(outbuf.at[i], backbuf.at[i], hb_s.at[i], hb_r.at[i], sibling if i == 4 else blk_at(d))
+        copy.start()
+        hbs.append(copy)
     for copy in xs:
         copy.wait_recv()
     total = x_in[0].astype(F32)
@@ -346,11 +354,6 @@
         copy = remote(xg.at[x], xg.at[x], xg_s.at[step], xg_r.at[step], x_at(step))
         copy.start()
         xgs.append(copy)
-    hbs = []
-    for i, d in hb_list:
-        copy = remote(outbuf.at[i], backbuf.at[i], hb_s.at[i], hb_r.at[i], sibling if i == 4 else blk_at(d))
-        copy.start()
-        hbs.append(copy)
     for copy in xgs:
         copy.wait_recv()
     yg[y] = xg[0:filled].reshape(piece_rows, TILE)

time: 78.4 us -> 77.6 us (0.990)
  no operation moved by 1% of the time
where the time goes in v5:
time: 77.6 us; the launch traced here: 77.4 us
  Pallas kernels  76.2 us (98%)
  between operations  1.29 us (2%)
    pallas_call x1, Pallas kernels, body(): pl.pallas_call(functools.partial(kernel, nodes, slots, reps), out_shape=(...  74.1 us
    pallas_call x1, Pallas kernels, body(): pl.pallas_call(finish, out_shape=(jax.ShapeDtypeStruct((rows, wide), BF16...  2.07 us

profile of v5, /device:TPU:1, one launch (start us, length us, event | category | flops | bytes accessed | tf_op | source)
XLA Modules:
  0.0 77.4 jit_solution(10831875680253720675)
XLA Ops:
  1.3 74.1 %shard_map.94 = (bf16[256,256]{1,0:T(8,128)(2,1)}, bf16[192,1024]{1,0:T(8,128)(2,1)}, bf16[192,256]{1,0:T(8,128)(2,1)}) custom-call(bf16[192,256]{1,0:T(8,128)(2,1)} %bitcast.2, bf16[768,1024]{1,0:T(8,128)(2,1)} %weight_hbm.1, bf16[256,256]{1,0:T(8,128)(2,1)} %cot_hbm.1, bf16[1,20,128,128]{3,2,1,0:T(8,128)(2,1)} %val_hbm.1, s32[1,20]{1,0:T(1,128)} %row_hbm.1, ...), custom_call_target="tpu_custom_call" | custom-call | tf_op jit(solution)/shard_map/pallas_call | solution.py:478
  75.4 2.1 %shard_map.95 = (bf16[256,256]{1,0:T(8,128)(2,1)}, f32[192,1024]{1,0:T(8,128)}, bf16[192,256]{1,0:T(8,128)(2,1)}) custom-call(bf16[256,256]{1,0:T(8,128)(2,1)} %get-tuple-element.9.hidden_in, bf16[192,1024]{1,0:T(8,128)(2,1)} %get-tuple-element.10.wgrad_in, bf16[192,256]{1,0:T(8,128)(2,1)} %get-tuple-element.11.fgrad_in), custom_call_target="tpu_custom_call" | custom-call | tf_op jit(solution)/shard_map/pallas_call | solution.py:492

commit v6 on v5

--- a/solution.py
+++ b/solution.py
@@ -278,20 +278,17 @@
         grad_at(n)
         weight_part(n, u, core_own)
 
-    def to_y(i):
-        where = {"blk": ((zl * NY + i) * NX + x) * NC + core}
-        return remote(y_out.at[i], y_in.at[y], y_s.at[i], y_r.at[y], where)
-
     for u in range(half):
         core_copies[u].wait_recv()
         for i in range(u * share, (u + 1) * share):
             total = core_own[i] + core_in[i].astype(F32)
             core_own[i] = total
             y_out[i] = total.astype(BF16)
-
-            @pl.when(y != i)
-            def _(i=i):
-                to_y(i).start()
+    ys = []
+    for step in (4, 3, 5, 2, 6, 1, 7) if NY == 8 else range(1, NY):
+        copy = remote(y_out.at[(y + step) % NY], y_in.at[y], y_s.at[step], y_r.at[step], y_at(step))
+        copy.start()
+        ys.append(copy)
 
     back_sum = mm_nt(weight[weight_rows(rep), 0:wide], grad[0])
     for n in range(1, groups):
@@ -322,9 +319,8 @@
     put_hidden.start()
 
     total = core_own[y]
-    for step in range(1, NY):
-        source = (y + step) % NY
-        remote(y_out.at[source], y_in.at[source], y_s.at[source], y_r.at[source], y_at(step)).wait_recv()
+    for copy in ys:
+        copy.wait_recv()
     for step in range(1, NY):
         total = total + y_in[(y + step) % NY].astype(F32)
     filled = piece_rows // x_rows
@@ -401,22 +397,33 @@
     put_hidden.wait()
     put_fgrad.wait()
     gathers = halo[0] + halo[1] + to_sibling[0] + to_sibling[1] + cots + aggs[0] + aggs[1] + relays
-    for i in range(NY):
-
-        @pl.when(y != i)
-        def _(i=i):
-            to_y(i).wait_send()
-
-    for copy in gathers + core_copies + hss + hbs + xs + xgs:
+    for copy in gathers + core_copies + ys + hss + hbs + xs + xgs:
         copy.wait_send()
     for _, copy in ygs:
         copy.wait_send()
 
 
-def finish(hidden_in, wgrad_in, fgrad_in, hidden_out, wgrad_out, fgrad_out):
-    hidden_out[...] = hidden_in[...]
-    fgrad_out[...] = fgrad_in[...]
-    wgrad_out[...] = wgrad_in[...].astype(F32)
+def finish(
+    hidden_in, wgrad_in, fgrad_in, hidden_out, wgrad_out, fgrad_out, hidden, fgrad, narrow, wgrad, in_sem, out_sem
+):
+    cuts = 4
+    depth = wgrad.shape[0] // cuts
+    parts = [pl.ds(i * depth, depth) for i in range(cuts)]
+    loads = [pltpu.make_async_copy(wgrad_in.at[at], narrow.at[at], in_sem.at[i]) for i, at in enumerate(parts)]
+    loads.append(pltpu.make_async_copy(hidden_in, hidden, in_sem.at[cuts]))
+    loads.append(pltpu.make_async_copy(fgrad_in, fgrad, in_sem.at[cuts + 1]))
+    for copy in loads:
+        copy.start()
+    stores = [pltpu.make_async_copy(wgrad.at[at], wgrad_out.at[at], out_sem.at[i]) for i, at in enumerate(parts)]
+    stores.append(pltpu.make_async_copy(hidden, hidden_out, out_sem.at[cuts]))
+    stores.append(pltpu.make_async_copy(fgrad, fgrad_out, out_sem.at[cuts + 1]))
+    for i in range(cuts + 2):
+        loads[i].wait()
+        if i < cuts:
+            wgrad[parts[i], :] = narrow[parts[i], :].astype(F32)
+        stores[i].start()
+    for copy in stores:
+        copy.wait()
 
 
 def body(features, weight, cotangent, tile_val, tile_row, tile_col, tile_count):
@@ -474,7 +481,6 @@
     ]
     anywhere = pl.BlockSpec(memory_space=pl.ANY)
     hbm = pl.BlockSpec(memory_space=pltpu.HBM)
-    whole = pl.BlockSpec(memory_space=pltpu.VMEM)
     results = pl.pallas_call(
         functools.partial(kernel, nodes, slots, reps),
         out_shape=(
@@ -496,8 +502,16 @@
             jax.ShapeDtypeStruct((panel, hid), F32),
             jax.ShapeDtypeStruct((panel, rows), BF16),
         ),
-        in_specs=[whole] * 3,
-        out_specs=(whole,) * 3,
+        in_specs=[hbm] * 3,
+        out_specs=(hbm,) * 3,
+        scratch_shapes=[
+            vmem((rows, wide), BF16),
+            vmem((panel, rows), BF16),
+            vmem((panel, hid), BF16),
+            vmem((panel, hid), F32),
+            dma((6,)),
+            dma((6,)),
+        ],
         compiler_params=pltpu.CompilerParams(vmem_limit_bytes=VMEM_BYTES),
     )(*results)
     return hidden, weight_grad, feature_grad.T

time: 77.6 us -> 76.1 us (0.981)
  Pallas kernels: 76.2 us -> 74.6 us
    pallas_call x1, Pallas kernels: 74.1 us -> 72.7 us  [body(): pl.pallas_call(functools.partial(kernel, nodes, slots, reps), out_shape=(...]
where the time goes in v6:
time: 76.1 us; the launch traced here: 75.9 us
  Pallas kernels  74.6 us (98%)
  between operations  1.29 us (2%)
    pallas_call x1, Pallas kernels, body(): pl.pallas_call(functools.partial(kernel, nodes, slots, reps), out_shape=(...  72.7 us
    pallas_call x1, Pallas kernels, body(): pl.pallas_call(finish, out_shape=(jax.ShapeDtypeStruct((rows, wide), BF16...  1.95 us

profile of v6, /device:TPU:1, one launch (start us, length us, event | category | flops | bytes accessed | tf_op | source)
XLA Modules:
  0.0 75.9 jit_solution(11423528237614301537)
XLA Ops:
  1.3 72.7 %shard_map.94 = (bf16[256,256]{1,0:T(8,128)(2,1)}, bf16[192,1024]{1,0:T(8,128)(2,1)}, bf16[192,256]{1,0:T(8,128)(2,1)}) custom-call(bf16[192,256]{1,0:T(8,128)(2,1)} %bitcast.2, bf16[768,1024]{1,0:T(8,128)(2,1)} %weight_hbm.1, bf16[256,256]{1,0:T(8,128)(2,1)} %cot_hbm.1, bf16[1,20,128,128]{3,2,1,0:T(8,128)(2,1)} %val_hbm.1, s32[1,20]{1,0:T(1,128)} %row_hbm.1, ...), custom_call_target="tpu_custom_call" | custom-call | tf_op jit(solution)/shard_map/pallas_call | solution.py:484
  73.9 2.0 %shard_map.95 = (bf16[256,256]{1,0:T(8,128)(2,1)}, f32[192,1024]{1,0:T(8,128)}, bf16[192,256]{1,0:T(8,128)(2,1)}) custom-call(bf16[256,256]{1,0:T(8,128)(2,1)} %get-tuple-element.9.hidden_in, bf16[192,1024]{1,0:T(8,128)(2,1)} %get-tuple-element.10.wgrad_in, bf16[192,256]{1,0:T(8,128)(2,1)} %get-tuple-element.11.fgrad_in), custom_call_target="tpu_custom_call" | custom-call | tf_op jit(solution)/shard_map/pallas_call | solution.py:498

commit v7 on v6

--- a/solution.py
+++ b/solution.py
@@ -313,11 +313,6 @@
         outbuf[i] = mine.astype(BF16)
     own_part[...] = mm(scaled, adj[REACH]) + back[...]
 
-    v = pre[rep]
-    hidden[...] = (v * jax.nn.sigmoid(v)).astype(BF16)
-    put_hidden = pltpu.make_async_copy(hidden, hidden_out, out_sem.at[0])
-    put_hidden.start()
-
     total = core_own[y]
     for copy in ys:
         copy.wait_recv()
@@ -339,6 +334,10 @@
         copy = remote(outbuf.at[i], backbuf.at[i], hb_s.at[i], hb_r.at[i], sibling if i == 4 else blk_at(d))
         copy.start()
         hbs.append(copy)
+    v = pre[rep]
+    hidden[...] = (v * jax.nn.sigmoid(v)).astype(BF16)
+    put_hidden = pltpu.make_async_copy(hidden, hidden_out, out_sem.at[0])
+    put_hidden.start()
     for copy in xs:
         copy.wait_recv()
     total = x_in[0].astype(F32)

time: 76.1 us -> 76.1 us (level)
  no operation moved by 1% of the time
where the time goes in v7:
time: 76.1 us; the launch traced here: 75.9 us
  Pallas kernels  74.6 us (98%)
  between operations  1.29 us (2%)
    pallas_call x1, Pallas kernels, body(): pl.pallas_call(functools.partial(kernel, nodes, slots, reps), out_shape=(...  72.7 us
    pallas_call x1, Pallas kernels, body(): pl.pallas_call(finish, out_shape=(jax.ShapeDtypeStruct((rows, wide), BF16...  1.95 us

profile of v7, /device:TPU:1, one launch (start us, length us, event | category | flops | bytes accessed | tf_op | source)
XLA Modules:
  0.0 75.9 jit_solution(16355990065162439129)
XLA Ops:
  1.3 72.7 %shard_map.94 = (bf16[256,256]{1,0:T(8,128)(2,1)}, bf16[192,1024]{1,0:T(8,128)(2,1)}, bf16[192,256]{1,0:T(8,128)(2,1)}) custom-call(bf16[192,256]{1,0:T(8,128)(2,1)} %bitcast.2, bf16[768,1024]{1,0:T(8,128)(2,1)} %weight_hbm.1, bf16[256,256]{1,0:T(8,128)(2,1)} %cot_hbm.1, bf16[1,20,128,128]{3,2,1,0:T(8,128)(2,1)} %val_hbm.1, s32[1,20]{1,0:T(1,128)} %row_hbm.1, ...), custom_call_target="tpu_custom_call" | custom-call | tf_op jit(solution)/shard_map/pallas_call | solution.py:483
  73.9 2.0 %shard_map.95 = (bf16[256,256]{1,0:T(8,128)(2,1)}, f32[192,1024]{1,0:T(8,128)}, bf16[192,256]{1,0:T(8,128)(2,1)}) custom-call(bf16[256,256]{1,0:T(8,128)(2,1)} %get-tuple-element.9.hidden_in, bf16[192,1024]{1,0:T(8,128)(2,1)} %get-tuple-element.10.wgrad_in, bf16[192,256]{1,0:T(8,128)(2,1)} %get-tuple-element.11.fgrad_in), custom_call_target="tpu_custom_call" | custom-call | tf_op jit(solution)/shard_map/pallas_call | solution.py:497
